TPU v7x, 128 devices: a whole 4x4x4 slice. The times are simulated.
128 devices in a mesh: step: 16 (over z, x), seq: 8 (over y, core).
Axes of the slice: x: 4, y: 4, z: 4, core: 2. Of those that a mesh axis runs over, the one named last changes fastest.
Arguments:
- start_state: float32 [1024, 1536], P('seq'), may hold values from -6 to 6
- timesteps: int32 [32], P('step'), may hold values from 0 to 999, as said below
- qkv_weight: bfloat16 [1536, 6144], replicated
- out_weight: bfloat16 [2048, 1536], P('seq'), may hold values from -0.5 to 0.5
Outputs:
- trajectory: float32 [32, 1024, 1536], P('step', 'seq')
Inputs may be any that keep to these rules, and one draw needn't show every extreme that they name: `timesteps`: distinct, falling along the steps, the first step at the maximum and the last at the minimum.
All inputs are finite; a program needn't handle non-finite values.
Results may differ from a plain program's by a relative error of at most 0.0029.
Values may be sent and summed in bfloat16 or wider, within the bound.
A program may use at most 128 MiB of HBM per device.

v0:
```python
import math

import jax
import jax.numpy as jnp
from jax import lax
from jax.sharding import PartitionSpec as P

HEAD_SIZE = 128
ITERS = 2


norm_eps = 1e-06


def entering(part, axis, combine, identity):
    place = lax.axis_index(axis)
    gathered = lax.all_gather(part, axis)
    state = jnp.zeros_like(part) + jnp.asarray(identity, part.dtype)

    def one(step, state):
        return combine(state, lax.dynamic_index_in_dim(gathered, step, 0, False))

    return lax.fori_loop(0, place, one, state)


def embed(step_index, model_width):
    half_width = model_width // 2
    frequency = jnp.exp(-math.log(10000.0) * jnp.arange(half_width, dtype=jnp.float32) / half_width)
    angles = step_index.astype(jnp.float32)[:, None] * frequency[None, :]
    return jnp.concatenate([jnp.sin(angles), jnp.cos(angles)], axis=1)


def attend(gathered):
    query_rows = gathered[:, :, 0]
    key_rows = gathered[:, :, 1]
    value_rows = gathered[:, :, 2]
    step_count, token_count, head_count, head_width = query_rows.shape
    block_rows = min(512, token_count)
    block_count = token_count // block_rows
    query_blocks = query_rows.reshape(step_count, block_count, block_rows, head_count, head_width)
    query_blocks = query_blocks.transpose(1, 0, 2, 3, 4)

    def one_block(query_piece):
        scores = jnp.einsum(
            "sqhd,skhd->shqk", query_piece, key_rows, preferred_element_type=jnp.float32
        )
        scores = scores * (1.0 / math.sqrt(head_width))
        peak = jnp.max(scores, axis=3, keepdims=True)
        expo = jnp.exp(scores - peak)
        softmax_total = jnp.sum(expo, axis=3, keepdims=True)
        softmax_weights = (expo / softmax_total).astype(jnp.bfloat16)
        return jnp.einsum(
            "shqk,skhd->sqhd", softmax_weights, value_rows, preferred_element_type=jnp.float32
        ).astype(jnp.bfloat16)

    outputs = lax.map(one_block, query_blocks)
    return outputs.transpose(1, 0, 2, 3, 4).reshape(step_count, token_count, head_count, head_width)


def on_device(start_state, timesteps, qkv_weight, out_weight):
    step_dev = timesteps.shape[0]
    tok_dev, model_width = start_state.shape
    head_total = qkv_weight.shape[1] // (3 * HEAD_SIZE)
    time_embed = embed(timesteps, model_width)
    step_scale = 1.0 / (step_dev * lax.axis_size("step"))
    whole_out = lax.all_gather(out_weight, "seq", axis=0, tiled=True)
    states = jnp.broadcast_to(start_state[None], (step_dev, tok_dev, model_width))
    result = states
    for round_index in range(ITERS):
        shifted = states + time_embed[:, None, :]
        mean_square = jnp.mean(shifted * shifted, axis=2, keepdims=True)
        normed = (shifted * lax.rsqrt(mean_square + norm_eps)).astype(jnp.bfloat16)
        projected = jnp.einsum(
            "std,dc->stc", normed, qkv_weight, preferred_element_type=jnp.float32
        ).astype(jnp.bfloat16)
        projected = projected.reshape(step_dev, tok_dev, 3, head_total, HEAD_SIZE)
        attended = attend(lax.all_to_all(projected, "seq", split_axis=3, concat_axis=1, tiled=True))
        by_token = lax.all_to_all(attended, "seq", split_axis=1, concat_axis=2, tiled=True)
        by_token = by_token.reshape(step_dev, tok_dev, head_total * HEAD_SIZE)
        drifts = jnp.einsum("stc,cd->std", by_token, whole_out, preferred_element_type=jnp.float32)
        inclusive = jnp.cumsum(drifts, axis=0)
        empty_total = jnp.zeros((tok_dev, model_width), jnp.float32)
        earlier = entering(inclusive[-1], "step", jnp.add, empty_total)
        if round_index == ITERS - 1:
            result = start_state[None] + step_scale * (earlier[None] + inclusive)
        else:
            local_before = jnp.concatenate(
                [jnp.zeros((1, tok_dev, model_width), jnp.float32), inclusive[:-1]], axis=0
            )
            states = start_state[None] + step_scale * (earlier[None] + local_before)
    return result


def solution(mesh):
    return jax.shard_map(
        on_device,
        mesh=mesh,
        in_specs=(P("seq", None), P("step"), P(), P("seq", None)),
        out_specs=P("step", "seq", None),
        check_vma=False,
    )
```

profile of v0, /device:TPU:103, one launch (start us, length us, event | category | flops | bytes accessed | tf_op | source)
XLA Modules:
  0.0 472.8 jit_solution(3083225086214400373)
XLA Ops:
  8.1 1.4 fusion.68
  9.5 12.1 %fusion.58 = bf16[2,128,6144]{2,1,0:T(8,128)(2,1)S(1)} fusion(bf16[1536,6144]{1,0:T(8,128)(2,1)} %param.14, f32[2,128]{1,0:T(2,128)S(1)} %add_rsqrt_fusion.1, f32[2,1536]{1,0:T(2,128)S(1)} %pad_maximum_fusion, f32[128,1536]{1,0:T(8,128)} %param.12), kind=kOutput, calls=%fused_computation.44 | convolution fusion | flops 4834590720 | bytes 22819840 | tf_op jit(solution)/shard_map/std,dc->stc/dot_general | solution.py:73
  22.3 2.5 copy.31
  24.8 5.1 %all-to-all-start = ((bf16[2,128,3,16,128]{4,1,2,0,3:T(8,128)(2,1)}), bf16[2,128,3,16,128]{4,1,2,0,3:T(8,128)(2,1)S(1)}, u32[]{:S(2)}, u32[]{:S(2)}) async-start(bf16[2,128,3,16,128]{4,1,2,0,3:T(8,128)(2,1)} %copy.31), calls=%async_computation | async-start | bytes 6291456 | tf_op jit(solution)/shard_map/all_to_all | solution.py:77
  29.9 53.6 %all-to-all-done = bf16[2,128,3,16,128]{4,1,2,0,3:T(8,128)(2,1)S(1)} async-done(((bf16[2,128,3,16,128]{4,1,2,0,3:T(8,128)(2,1)}), bf16[2,128,3,16,128]{4,1,2,0,3:T(8,128)(2,1)S(1)}, u32[]{:S(2)}, u32[]{:S(2)}) %all-to-all-start) | async-done | bytes 3145760 | tf_op jit(solution)/shard_map/all_to_all | solution.py:77
  83.8 1.2 slice_bitcast_fusion.2
  85.2 23.6 %while.40 = (s32[]{:T(128)}, bf16[2,2,512,2,128]{4,2,0,3,1:T(8,128)(2,1)S(1)}, bf16[2,2,512,2,128]{4,2,3,1,0:T(8,128)(2,1)S(1)}, bf16[2,1024,2,128]{3,1,2,0:T(8,...) while((s32[]{:T(128)}, bf16[2,2,512,2,128]{4,2,0,3,1:T(8,128)(2,1)S(1)}, ...), condition=%wide.region_4.5_spmd, body=%wide.region_1.4_spmd.sunk | while | flops 1084490752 | bytes 19939404 | solution.py:56
  85.2 7.0 %fusion.117 = (f32[2,2,512]{2,1,0:T(2,128)S(1)}, f32[2,2,512,1024]{3,2,1,0:T(8,128)}) fusion(bf16[2,1024,2,128]{3,1,2,0:T(8,128)(2,1)} %get-tuple-element.296, bf16[2,2,512,2,128]{4,2,3,1,0:T(8,128)(2,1)S(1)} %get-tuple-element.295, s32[]{:T(128)} %get-tuple-element.287), kind=kOutput, calls=%fused_computation.80.clone.1 | convolution fusion | flops 543163392 | bytes 9969668 | tf_op jit(solution)/shard_map/while/body/eval_jaxpr/sub | solution.py:49
  92.2 4.8 %fusion.118 = bf16[2,2,512,2,128]{4,2,0,3,1:T(8,128)(2,1)S(1)} fusion(bf16[2,2,512,2,128]{4,2,0,3,1:T(8,128)(2,1)S(1)} %get-tuple-element.288, s32[]{:T(128)} %get-tuple-element.287, bf16[2,1024,2,128]{3,1,2,0:T(8,128)(2,1)S(1)} %get-tuple-element.297, f32[2,2,512,1024]{3,2,1,0:T(8,128)} %get-tuple-element.264, f32[2,2,512]{2,1,0:T(2,128)S(1)} %get-tuple-element.265), kind=kOutput, calls=%fused_computation.9.clone.1 | convolution fusion | flops 541327360 | bytes 9969668 | tf_op jit(solution)/shard_map/while/body/eval_jaxpr/shqk,skhd->sqhd/dot_general | solution.py:52
  97.0 7.0 %fusion.117 = (f32[2,2,512]{2,1,0:T(2,128)S(1)}, f32[2,2,512,1024]{3,2,1,0:T(8,128)}) fusion(bf16[2,1024,2,128]{3,1,2,0:T(8,128)(2,1)} %get-tuple-element.296, bf16[2,2,512,2,128]{4,2,3,1,0:T(8,128)(2,1)S(1)} %get-tuple-element.295, s32[]{:T(128)} %get-tuple-element.287), kind=kOutput, calls=%fused_computation.80.clone.1 | convolution fusion | flops 543163392 | bytes 9969668 | tf_op jit(solution)/shard_map/while/body/eval_jaxpr/sub | solution.py:49
  104.0 4.8 %fusion.118 = bf16[2,2,512,2,128]{4,2,0,3,1:T(8,128)(2,1)S(1)} fusion(bf16[2,2,512,2,128]{4,2,0,3,1:T(8,128)(2,1)S(1)} %get-tuple-element.288, s32[]{:T(128)} %get-tuple-element.287, bf16[2,1024,2,128]{3,1,2,0:T(8,128)(2,1)S(1)} %get-tuple-element.297, f32[2,2,512,1024]{3,2,1,0:T(8,128)} %get-tuple-element.264, f32[2,2,512]{2,1,0:T(2,128)S(1)} %get-tuple-element.265), kind=kOutput, calls=%fused_computation.9.clone.1 | convolution fusion | flops 541327360 | bytes 9969668 | tf_op jit(solution)/shard_map/while/body/eval_jaxpr/shqk,skhd->sqhd/dot_general | solution.py:52
  108.8 1.1 copy.35
  109.9 18.3 %all_to_all.66 = bf16[2,1024,2,128]{3,2,0,1:T(2,128)(2,1)S(1)} all-to-all(bf16[2,1024,2,128]{3,2,0,1:T(2,128)(2,1)S(1)} %copy.35), channel_id=1, replica_groups=mesh['step'=16,'seq'=8] {'seq'}, dimensions={1} | all-to-all | bytes 2097152 | tf_op jit(solution)/shard_map/all_to_all | solution.py:78
  128.4 1.1 copy.37
  130.3 4.6 fusion.66
  136.9 88.0 %all-gather.6.cloned.1.call-done = f32[16,128,1536]{2,1,0:T(8,128)} async-done(((f32[1,128,1536]{2,1,0:T(8,128)}), f32[16,128,1536]{2,1,0:T(8,128)}) %all-gather.6.cloned.1.call-update) | async-done | bytes 12582928 | tf_op jit(solution)/shard_map/all_gather | solution.py:17
  225.0 20.5 %while.41 = (s32[]{:T(128)}, f32[128,1536]{1,0:T(8,128)S(1)}, s32[]{:T(128)}, f32[16,128,1536]{2,1,0:T(8,128)}, s32[]{:T(128)}, /*index=5*/s32[]{:T(128)}, s32[]{:T(128)}) while((s32[]{:T(128)}, f32[128,1536]{1,0:T(8,128)S(1)}, s32[]{:T(128)}, f32[16,128,1536]{2,1,0:T(8,128)}, s32[]{:T(128)}, /*index=5*/s32[]{:T(128)}, s32[]{:T(128)}) %tuple.72), condition=%wide.region_7.8_spmd, body=%wide.region_6.7_spmd.sunk | while | flops 196613 | bytes 2359411 | solution.py:23
  225.0 1.4 bitcast_add_fusion.4
  226.4 1.3 bitcast_add_fusion.4
  227.8 1.3 bitcast_add_fusion.4
  229.2 1.3 bitcast_add_fusion.4
  230.5 1.3 bitcast_add_fusion.4
  231.9 1.3 bitcast_add_fusion.4
  233.2 1.3 bitcast_add_fusion.4
  234.6 1.3 bitcast_add_fusion.4
  236.0 1.3 bitcast_add_fusion.4
  237.3 1.3 bitcast_add_fusion.4
  238.7 1.3 bitcast_add_fusion.4
  240.0 1.3 bitcast_add_fusion.4
  241.4 1.3 bitcast_add_fusion.4
  242.7 1.3 bitcast_add_fusion.4
  244.1 1.3 bitcast_add_fusion.4
  245.8 11.9 %fusion.61 = bf16[2,128,6144]{2,1,0:T(8,128)(2,1)S(1)} fusion(bf16[1536,6144]{1,0:T(8,128)(2,1)} %param.14, f32[1,128,1536]{2,1,0:T(8,128)S(1)} %get-tuple-element.156, f32[2,128]{1,0:T(2,128)S(1)} %add_rsqrt_fusion, f32[128,1536]{1,0:T(8,128)S(1)} %get-tuple-element.106, f32[2,1536]{1,0:T(2,128)S(1)} %pad_maximum_fusion, f32[128,1536]{1,0:T(8,128)S(1)} %copy-done), kind=kOutput, calls=%fused_computation.45 | convolution fusion | flops 4835770368 | bytes 24392704 | tf_op jit(solution)/shard_map/std,dc->stc/dot_general | solution.py:73
  258.5 2.5 copy.38
  261.0 5.0 %all-to-all-start.2 = ((bf16[2,128,3,16,128]{4,1,2,0,3:T(8,128)(2,1)}), bf16[2,128,3,16,128]{4,1,2,0,3:T(8,128)(2,1)S(1)}, u32[]{:S(2)}, u32[]{:S(2)}) async-start(bf16[2,128,3,16,128]{4,1,2,0,3:T(8,128)(2,1)} %copy.38), calls=%async_computation.2 | async-start | bytes 6291456 | tf_op jit(solution)/shard_map/all_to_all | solution.py:77
  265.9 37.6 %all-to-all-done.2 = bf16[2,128,3,16,128]{4,1,2,0,3:T(8,128)(2,1)S(1)} async-done(((bf16[2,128,3,16,128]{4,1,2,0,3:T(8,128)(2,1)}), bf16[2,128,3,16,128]{4,1,2,0,3:T(8,128)(2,1)S(1)}, u32[]{:S(2)}, u32[]{:S(2)}) %all-to-all-start.2) | async-done | bytes 3145760 | tf_op jit(solution)/shard_map/all_to_all | solution.py:77
  303.7 1.2 slice_bitcast_fusion
  305.2 23.6 %while.42 = (s32[]{:T(128)}, bf16[2,2,512,2,128]{4,2,0,3,1:T(8,128)(2,1)S(1)}, bf16[2,2,512,2,128]{4,2,3,1,0:T(8,128)(2,1)S(1)}, bf16[2,1024,2,128]{3,1,2,0:T(8,...) while((s32[]{:T(128)}, bf16[2,2,512,2,128]{4,2,0,3,1:T(8,128)(2,1)S(1)}, ...), condition=%wide.region_12.13_spmd, body=%wide.region_9.12_spmd.sunk | while | flops 1084490752 | bytes 19939404 | solution.py:56
  305.2 7.0 %fusion.122 = (f32[2,2,512]{2,1,0:T(2,128)S(1)}, f32[2,2,512,1024]{3,2,1,0:T(8,128)}) fusion(bf16[2,1024,2,128]{3,1,2,0:T(8,128)(2,1)} %get-tuple-element.335, bf16[2,2,512,2,128]{4,2,3,1,0:T(8,128)(2,1)S(1)} %get-tuple-element.334, s32[]{:T(128)} %get-tuple-element.326), kind=kOutput, calls=%fused_computation.81.clone.1 | convolution fusion | flops 543163392 | bytes 9969668 | tf_op jit(solution)/shard_map/while/body/eval_jaxpr/sub | solution.py:49
  312.2 4.8 %fusion.123 = bf16[2,2,512,2,128]{4,2,0,3,1:T(8,128)(2,1)S(1)} fusion(bf16[2,2,512,2,128]{4,2,0,3,1:T(8,128)(2,1)S(1)} %get-tuple-element.327, s32[]{:T(128)} %get-tuple-element.326, bf16[2,1024,2,128]{3,1,2,0:T(8,128)(2,1)S(1)} %get-tuple-element.336, f32[2,2,512,1024]{3,2,1,0:T(8,128)} %get-tuple-element.275, f32[2,2,512]{2,1,0:T(2,128)S(1)} %get-tuple-element.276), kind=kOutput, calls=%fused_computation.29.clone.1 | convolution fusion | flops 541327360 | bytes 9969668 | tf_op jit(solution)/shard_map/while/body/eval_jaxpr/shqk,skhd->sqhd/dot_general | solution.py:52
  317.0 7.0 %fusion.122 = (f32[2,2,512]{2,1,0:T(2,128)S(1)}, f32[2,2,512,1024]{3,2,1,0:T(8,128)}) fusion(bf16[2,1024,2,128]{3,1,2,0:T(8,128)(2,1)} %get-tuple-element.335, bf16[2,2,512,2,128]{4,2,3,1,0:T(8,128)(2,1)S(1)} %get-tuple-element.334, s32[]{:T(128)} %get-tuple-element.326), kind=kOutput, calls=%fused_computation.81.clone.1 | convolution fusion | flops 543163392 | bytes 9969668 | tf_op jit(solution)/shard_map/while/body/eval_jaxpr/sub | solution.py:49
  324.0 4.8 %fusion.123 = bf16[2,2,512,2,128]{4,2,0,3,1:T(8,128)(2,1)S(1)} fusion(bf16[2,2,512,2,128]{4,2,0,3,1:T(8,128)(2,1)S(1)} %get-tuple-element.327, s32[]{:T(128)} %get-tuple-element.326, bf16[2,1024,2,128]{3,1,2,0:T(8,128)(2,1)S(1)} %get-tuple-element.336, f32[2,2,512,1024]{3,2,1,0:T(8,128)} %get-tuple-element.275, f32[2,2,512]{2,1,0:T(2,128)S(1)} %get-tuple-element.276), kind=kOutput, calls=%fused_computation.29.clone.1 | convolution fusion | flops 541327360 | bytes 9969668 | tf_op jit(solution)/shard_map/while/body/eval_jaxpr/shqk,skhd->sqhd/dot_general | solution.py:52
  328.8 1.1 copy.42
  329.9 18.4 %all_to_all.67 = bf16[2,1024,2,128]{3,2,0,1:T(2,128)(2,1)S(1)} all-to-all(bf16[2,1024,2,128]{3,2,0,1:T(2,128)(2,1)S(1)} %copy.42), channel_id=1, replica_groups=mesh['step'=16,'seq'=8] {'seq'}, dimensions={1} | all-to-all | bytes 2097152 | tf_op jit(solution)/shard_map/all_to_all | solution.py:78
  348.4 1.1 copy.44
  350.3 4.6 fusion.64
  356.8 87.5 %all-gather.8.cloned.1.call-done = f32[16,128,1536]{2,1,0:T(8,128)} async-done(((f32[1,128,1536]{2,1,0:T(8,128)}), f32[16,128,1536]{2,1,0:T(8,128)}) %all-gather.8.cloned.1.call-update) | async-done | bytes 12582928 | tf_op jit(solution)/shard_map/all_gather | solution.py:17
  444.4 20.5 %while.43 = (s32[]{:T(128)}, f32[128,1536]{1,0:T(8,128)S(1)}, s32[]{:T(128)}, f32[16,128,1536]{2,1,0:T(8,128)}, s32[]{:T(128)}, /*index=5*/s32[]{:T(128)}, s32[]{:T(128)}) while((s32[]{:T(128)}, f32[128,1536]{1,0:T(8,128)S(1)}, s32[]{:T(128)}, f32[16,128,1536]{2,1,0:T(8,128)}, s32[]{:T(128)}, /*index=5*/s32[]{:T(128)}, s32[]{:T(128)}) %tuple.78), condition=%wide.region_15.16_spmd, body=%wide.region_14.15_spmd.sunk | while | flops 196613 | bytes 2359411 | solution.py:23
  444.4 1.4 bitcast_add_fusion.5
  445.8 1.3 bitcast_add_fusion.5
  447.2 1.3 bitcast_add_fusion.5
  448.6 1.3 bitcast_add_fusion.5
  449.9 1.3 bitcast_add_fusion.5
  451.3 1.3 bitcast_add_fusion.5
  452.6 1.3 bitcast_add_fusion.5
  454.0 1.3 bitcast_add_fusion.5
  455.4 1.3 bitcast_add_fusion.5
  456.7 1.3 bitcast_add_fusion.5
  458.1 1.3 bitcast_add_fusion.5
  459.4 1.3 bitcast_add_fusion.5
  460.8 1.3 bitcast_add_fusion.5
  462.2 1.3 bitcast_add_fusion.5
  463.5 1.3 bitcast_add_fusion.5
  464.9 1.4 multiply_add_fusion
  (36 shorter events, 10.3 us)
Async XLA Ops:
  6.5 123.8 %all-gather.4.cloned.1.call-start = ((), (), s32[]{:S(2)}) async-start(), calls=%async_computation.4 | async-start | bytes 7077888 | tf_op jit(solution)/shard_map/all_gather | solution.py:66
  24.8 58.7 %all-to-all-start = ((bf16[2,128,3,16,128]{4,1,2,0,3:T(8,128)(2,1)}), bf16[2,128,3,16,128]{4,1,2,0,3:T(8,128)(2,1)S(1)}, u32[]{:S(2)}, u32[]{:S(2)}) async-start(bf16[2,128,3,16,128]{4,1,2,0,3:T(8,128)(2,1)} %copy.31), calls=%async_computation | async-start | bytes 6291456 | tf_op jit(solution)/shard_map/all_to_all | solution.py:77
  29.9 195.0 %all-gather.6.cloned.1.call-start = ((), (), s32[]{:S(2)}) async-start(), calls=%async_computation.5 | async-start | bytes 13369344 | tf_op jit(solution)/shard_map/all_gather | solution.py:17
  225.0 20.5 %copy-start = (f32[128,1536]{1,0:T(8,128)S(1)}, f32[128,1536]{1,0:T(8,128)}, u32[]{:S(2)}) copy-start(f32[128,1536]{1,0:T(8,128)} %param.12) | copy-start | bytes 2359300
  261.0 42.5 %all-to-all-start.2 = ((bf16[2,128,3,16,128]{4,1,2,0,3:T(8,128)(2,1)}), bf16[2,128,3,16,128]{4,1,2,0,3:T(8,128)(2,1)S(1)}, u32[]{:S(2)}, u32[]{:S(2)}) async-start(bf16[2,128,3,16,128]{4,1,2,0,3:T(8,128)(2,1)} %copy.38), calls=%async_computation.2 | async-start | bytes 6291456 | tf_op jit(solution)/shard_map/all_to_all | solution.py:77
  265.9 178.4 %all-gather.8.cloned.1.call-start = ((), (), s32[]{:S(2)}) async-start(), calls=%async_computation.6 | async-start | bytes 13369344 | tf_op jit(solution)/shard_map/all_gather | solution.py:17
  444.4 20.5 %copy-start.1 = (f32[128,1536]{1,0:T(8,128)S(1)}, f32[128,1536]{1,0:T(8,128)}, u32[]{:S(2)}) copy-start(f32[128,1536]{1,0:T(8,128)} %param.12) | copy-start | bytes 2359300
Sparse Core Ops, SparseCore 0:
  9.0 65.4 all-gather.3
  137.0 87.8 all-gather.5
  356.9 87.3 all-gather.7
where the time goes:
time: 475 us; the launch traced here: 473 us
  waiting for transfers between devices  267 us (56%)
  matrix products  80.2 us (17%)
  other arithmetic  46.1 us (10%)
  blocking collectives  36.7 us (8%)
  local copies, waits for them, and re-layouts  18 us (4%)
  between operations  13.4 us (3%)
  starting transfers between devices  10.1 us (2%)
    all_gather x2, waiting for transfers between devices, entering(): gathered = lax.all_gather(part, axis)  175 us
    all_to_all x2, waiting for transfers between devices, on_device(): lax.all_to_all(projected, 'seq', split_axis=3, concat_axis=1, tiled=True)  91.2 us
    add x30, other arithmetic, one(): return combine(state, lax.dynamic_index_in_dim(gathered, step, 0, False))  40.1 us
    all_to_all x2, blocking collectives, on_device(): lax.all_to_all(attended, 'seq', split_axis=1, concat_axis=2, tiled=True)  36.7 us
    sub x4, matrix products, one_block(): expo = jnp.exp(scores - peak)  28 us
    dot_general x2, matrix products, on_device(): jnp.einsum('std,dc->stc', normed, qkv_weight, preferred_element_type=jnp....  24 us
    dot_general x4, matrix products, one_block(): jnp.einsum('shqk,skhd->sqhd', softmax_weights, value_rows, preferred_elem...  19.1 us
    all_to_all x2, starting transfers between devices, on_device(): lax.all_to_all(projected, 'seq', split_axis=3, concat_axis=1, tiled=True)  10.1 us
  transfers between devices with their start and end apart: 5, of which 4 were waited for; matrix products, arithmetic and copies ran while one was open for 10% of the time, Pallas kernels for 0%

commit v1 on v0

v1 whole, which is shorter than its diff:
```python
import functools
import math

import jax
import jax.numpy as jnp
from jax import lax
from jax.experimental import pallas as pl
from jax.experimental.pallas import tpu as pltpu
from jax.sharding import PartitionSpec as P

HEAD_SIZE = 128
HEADS = 16
ITERS = 2
NORM_EPS = 1e-06
MESH = pl.DeviceIdType.MESH
F32 = jnp.float32
BF16 = jnp.bfloat16


def embed(step_index, model_width):
    half_width = model_width // 2
    frequency = jnp.exp(-math.log(10000.0) * jnp.arange(half_width, dtype=F32) / half_width)
    angles = step_index.astype(F32)[:, None] * frequency[None, :]
    return jnp.concatenate([jnp.sin(angles), jnp.cos(angles)], axis=1)


def kernel(
    n_step,
    start_ref, te_ref, wqkv_ref, wout_ref,
    out_ref,
    w_ref, wo_ref, x_ref, ns_ref, qkv_ref, att_ref, recv_ref, dr_ref, bs_ref, pr_ref, pe_ref, e_ref, pf_ref, ef_ref,
    w_sem, wo_sem, wo_send, wo_recv, wo_fsend, wo_frecv,
    x_send, x_recv, x_fsend, x_frecv,
    a_sem, a_send, a_recv,
    p_send, p_recv, e_send, e_recv,
):
    tok, width = start_ref.shape
    total_tok = 8 * tok
    group = HEADS // 4
    gw = group * HEAD_SIZE
    inner = HEADS * HEAD_SIZE
    n_total = 2 * n_step
    s = lax.axis_index("step")
    q = lax.axis_index("seq")
    y, c = q // 2, q % 2
    j = y // 2
    g = (y % 2) * 2 + c
    row_parts = min(n_step, 8)
    lane_parts = n_step // row_parts
    prow, plane = tok // row_parts, width // lane_parts
    scale = 1.0 / n_total

    w_copies = []
    for part in range(3):
        w_copies.append(pltpu.make_async_copy(
            wqkv_ref.at[:, pl.ds(pl.multiple_of(part * inner + g * gw, 128), gw)],
            w_ref.at[:, pl.ds(part * gw, gw)],
            w_sem.at[part]))
        w_copies[-1].start()
    orow = wout_ref.shape[0]
    wo_own = pltpu.make_async_copy(
        wout_ref, wo_ref.at[pl.ds(pl.multiple_of(q * orow, orow), orow)], wo_sem)
    wo_own.start()

    barrier = pltpu.get_barrier_semaphore()
    for k in range(1, 8):
        pl.semaphore_signal(barrier, inc=1, device_id=(s, lax.rem(q + k, 8)), device_id_type=MESH)
    for k in range(1, n_step):
        pl.semaphore_signal(barrier, inc=1, device_id=(lax.rem(s + k, n_step), q), device_id_type=MESH)
    pl.semaphore_wait(barrier, 7 + n_step - 1)

    def other(dy):
        return lax.rem(y + dy, 4)

    def wo_rows(ref, qq):
        return ref.at[pl.ds(pl.multiple_of(qq * orow, orow), orow)]

    def wo_copy(dy):
        return pltpu.make_async_remote_copy(
            src_ref=wout_ref, dst_ref=wo_rows(wo_ref, q),
            send_sem=wo_send.at[dy - 1], recv_sem=wo_recv.at[dy - 1],
            device_id=(s, 2 * other(dy) + c), device_id_type=MESH)

    def wo_arrival(dy):
        src = 2 * other(4 - dy) + c
        return pltpu.make_async_remote_copy(
            src_ref=wout_ref, dst_ref=wo_rows(wo_ref, src),
            send_sem=wo_send.at[dy - 1], recv_sem=wo_recv.at[dy - 1],
            device_id=(s, q), device_id_type=MESH)

    def wo_forward(dy):
        src = 2 * other(4 - dy) + c
        return pltpu.make_async_remote_copy(
            src_ref=wo_rows(wo_ref, src), dst_ref=wo_rows(wo_ref, src),
            send_sem=wo_fsend.at[dy % 4], recv_sem=wo_frecv.at[dy % 4],
            device_id=(s, 2 * y + 1 - c), device_id_type=MESH)

    def wo_forwarded(dy):
        src = 2 * other(4 - dy) + 1 - c
        return pltpu.make_async_remote_copy(
            src_ref=wo_rows(wo_ref, src), dst_ref=wo_rows(wo_ref, src),
            send_sem=wo_fsend.at[dy % 4], recv_sem=wo_frecv.at[dy % 4],
            device_id=(s, 2 * y + 1 - c), device_id_type=MESH)

    def x_rows(qq):
        return x_ref.at[pl.ds(pl.multiple_of(qq * tok, tok), tok)]

    def x_copy(dy):
        dest = other(dy)
        return pltpu.make_async_remote_copy(
            src_ref=ns_ref.at[dest // 2], dst_ref=x_rows(q),
            send_sem=x_send.at[dy - 1], recv_sem=x_recv.at[dy - 1],
            device_id=(s, 2 * dest + c), device_id_type=MESH)

    def x_arrival(dy):
        return pltpu.make_async_remote_copy(
            src_ref=ns_ref.at[0], dst_ref=x_rows(2 * other(4 - dy) + c),
            send_sem=x_send.at[dy - 1], recv_sem=x_recv.at[dy - 1],
            device_id=(s, q), device_id_type=MESH)

    def x_forward(dy):
        src = 2 * other(4 - dy) + c
        return pltpu.make_async_remote_copy(
            src_ref=x_rows(src), dst_ref=x_rows(src),
            send_sem=x_fsend.at[dy % 4], recv_sem=x_frecv.at[dy % 4],
            device_id=(s, 2 * y + 1 - c), device_id_type=MESH)

    def x_forwarded(dy):
        src = 2 * other(4 - dy) + 1 - c
        return pltpu.make_async_remote_copy(
            src_ref=x_rows(src), dst_ref=x_rows(src),
            send_sem=x_fsend.at[dy % 4], recv_sem=x_frecv.at[dy % 4],
            device_id=(s, 2 * y + 1 - c), device_id_type=MESH)

    def piece(ref, who):
        return ref.at[pl.ds(pl.multiple_of((who // lane_parts) * prow, prow), prow),
                      pl.ds(pl.multiple_of((who % lane_parts) * plane, 128), plane)]

    def put_normed(i, state):
        shifted = state + te_ref[i:i + 1, :]
        mean_square = jnp.mean(shifted * shifted, axis=1, keepdims=True)
        ns_ref[i] = (shifted * lax.rsqrt(mean_square + NORM_EPS)).astype(BF16)

    def project(yy):
        rows = pl.ds(pl.multiple_of(yy * 2 * tok, 2 * tok), 2 * tok)

        def columns(n, _):
            cols = pl.ds(pl.multiple_of(n * gw, gw), gw)
            factor = jnp.where(n == 0, math.log2(math.e) / math.sqrt(HEAD_SIZE), 1.0)
            qkv_ref[rows, cols] = (jnp.dot(
                x_ref[rows, :], w_ref[:, cols], preferred_element_type=F32) * factor).astype(BF16)
            return 0

        lax.fori_loop(0, 3, columns, 0)

    def attend(yy):
        start_row = pl.multiple_of(yy * 2 * tok, 2 * tok)
        rows = pl.ds(start_row, 2 * tok)

        def head(h, _):
            def cols(part):
                return pl.ds(pl.multiple_of(part * gw + h * HEAD_SIZE, HEAD_SIZE), HEAD_SIZE)

            scores = lax.dot_general(
                qkv_ref[rows, cols(0)], qkv_ref[:, cols(1)],
                (((1,), (1,)), ((), ())), preferred_element_type=F32)
            peak = jnp.max(scores, axis=1, keepdims=True)
            expo = jnp.exp2(scores - peak)
            total = jnp.sum(expo, axis=1, keepdims=True)
            mixed = jnp.dot(expo.astype(BF16), qkv_ref[:, cols(2)], preferred_element_type=F32)
            att_ref[rows, cols(0)] = (mixed / total).astype(BF16)
            return 0

        lax.fori_loop(0, group, head, 0)

    def recv_block(qq):
        yy, cc = qq // 2, qq % 2
        return recv_ref.at[pl.ds(pl.multiple_of((yy // 2) * tok, tok), tok),
                           pl.ds(pl.multiple_of(((yy % 2) * 2 + cc) * gw, gw), gw)]

    def att_rows(qq):
        return att_ref.at[pl.ds(pl.multiple_of(qq * tok, tok), tok)]

    def a_copy(dy, dc):
        dest = 2 * other(dy) + lax.rem(c + dc, 2)
        return pltpu.make_async_remote_copy(
            src_ref=att_rows(dest), dst_ref=recv_block(q),
            send_sem=a_send.at[2 * dy + dc - 1], recv_sem=a_recv.at[2 * dy + dc - 1],
            device_id=(s, dest), device_id_type=MESH)

    def a_arrival(dy, dc):
        src = 2 * other(4 - dy) + lax.rem(c + dc, 2)
        return pltpu.make_async_remote_copy(
            src_ref=att_rows(q), dst_ref=recv_block(src),
            send_sem=a_send.at[2 * dy + dc - 1], recv_sem=a_recv.at[2 * dy + dc - 1],
            device_id=(s, q), device_id_type=MESH)

    def step_peer(k):
        return lax.rem(s + k, n_step)

    for it in range(ITERS):
        if it == 0:
            for i in range(2):
                put_normed(i, start_ref[...])
        else:
            before = e_ref[...].astype(F32)
            put_normed(0, start_ref[...] + scale * before)
            put_normed(1, start_ref[...] + scale * (before + dr_ref[0]))

        for dy in (2, 1, 3):
            x_copy(dy).start()
        x_rows(q)[...] = ns_ref[j]
        x_forward(0).start()
        if it == 0:
            for dy in (2, 1, 3):
                wo_copy(dy).start()
            for copy in w_copies:
                copy.wait()
        x_forwarded(0).wait_recv()
        project(y)
        for dy in (1, 3, 2):
            x_arrival(dy).wait_recv()
            x_forward(dy).start()
            x_forwarded(dy).wait_recv()
            project(other(4 - dy))
        for dy in (1, 2, 3):
            x_copy(dy).wait_send()
        for dy in range(4):
            x_forward(dy).wait_send()

        for dy in (2, 1, 3, 0):
            attend(other(dy))
            for dc in (0, 1):
                if dy == 0 and dc == 0:
                    own = pltpu.make_async_copy(att_rows(q), recv_block(q), a_sem)
                    own.start()
                else:
                    a_copy(dy, dc).start()
        if it == 0:
            wo_own.wait()
            wo_forward(0).start()
            for dy in (1, 3, 2):
                wo_arrival(dy).wait_recv()
                wo_forward(dy).start()
            for dy in range(4):
                wo_forwarded(dy).wait_recv()
            for dy in (1, 2, 3):
                wo_copy(dy).wait_send()
            for dy in range(4):
                wo_forward(dy).wait_send()
        own.wait()
        for n in range(1, 8):
            a_arrival(n // 2, n % 2).wait_recv()
        for n in range(1, 8):
            a_copy(n // 2, n % 2).wait_send()

        def drift(n, _):
            cols = pl.ds(pl.multiple_of(n * 256, 256), 256)
            both = jnp.dot(recv_ref[...], wo_ref[:, cols], preferred_element_type=F32)
            first, second = both[:tok], both[tok:]
            dr_ref[0, :, cols] = first
            dr_ref[1, :, cols] = first + second
            bs_ref[:, cols] = (first + second).astype(BF16)
            return 0

        lax.fori_loop(0, width // 256, drift, 0)

        pieces, sums = (pe_ref, e_ref) if it < ITERS - 1 else (pf_ref, ef_ref)

        def p_copy(k):
            dest = step_peer(k)
            return pltpu.make_async_remote_copy(
                src_ref=piece(bs_ref, dest), dst_ref=pr_ref.at[s],
                send_sem=p_send.at[k - 1], recv_sem=p_recv.at[k - 1],
                device_id=(dest, q), device_id_type=MESH)

        def p_arrival(k):
            return pltpu.make_async_remote_copy(
                src_ref=piece(bs_ref, s), dst_ref=pr_ref.at[step_peer(n_step - k)],
                send_sem=p_send.at[k - 1], recv_sem=p_recv.at[k - 1],
                device_id=(s, q), device_id_type=MESH)

        def e_copy(k):
            dest = step_peer(k)
            return pltpu.make_async_remote_copy(
                src_ref=pieces.at[dest], dst_ref=piece(sums, s),
                send_sem=e_send.at[k - 1], recv_sem=e_recv.at[k - 1],
                device_id=(dest, q), device_id_type=MESH)

        def e_arrival(k):
            return pltpu.make_async_remote_copy(
                src_ref=pieces.at[s], dst_ref=piece(sums, step_peer(n_step - k)),
                send_sem=e_send.at[k - 1], recv_sem=e_recv.at[k - 1],
                device_id=(s, q), device_id_type=MESH)

        for k in range(1, n_step):
            p_copy(k).start()
        pr_ref[s] = piece(bs_ref, s)[...]
        for k in range(1, n_step):
            p_arrival(k).wait_recv()

        def prefix(k, total):
            pieces[k] = total.astype(pieces.dtype)
            return total + pr_ref[k].astype(F32)

        lax.fori_loop(0, n_step, prefix, jnp.zeros((prow, plane), F32))
        for k in range(1, n_step):
            e_copy(k).start()
        piece(sums, s)[...] = pieces[s]
        for k in range(1, n_step):
            e_arrival(k).wait_recv()
        for k in range(1, n_step):
            p_copy(k).wait_send()
            e_copy(k).wait_send()

    before = ef_ref[...]
    for i in range(2):
        out_ref[i] = before + dr_ref[i]


def on_device(n_step, start_state, timesteps, qkv_weight, out_weight):
    tok, width = start_state.shape
    inner = HEADS * HEAD_SIZE
    te = embed(timesteps, width)
    row_parts = min(n_step, 8)
    lane_parts = n_step // row_parts
    prow, plane = tok // row_parts, width // lane_parts
    dma = pltpu.SemaphoreType.DMA
    vmem = pl.BlockSpec(memory_space=pltpu.VMEM)
    hbm = pl.BlockSpec(memory_space=pl.ANY)
    sums = pl.pallas_call(
        functools.partial(kernel, n_step),
        out_shape=jax.ShapeDtypeStruct((2, tok, width), F32),
        in_specs=[vmem, vmem, hbm, vmem],
        out_specs=vmem,
        scratch_shapes=[
            pltpu.VMEM((width, 3 * inner // 4), BF16),
            pltpu.VMEM((inner, width), BF16),
            pltpu.VMEM((8 * tok, width), BF16),
            pltpu.VMEM((2, tok, width), BF16),
            pltpu.VMEM((8 * tok, 3 * inner // 4), BF16),
            pltpu.VMEM((8 * tok, inner // 4), BF16),
            pltpu.VMEM((2 * tok, inner), BF16),
            pltpu.VMEM((2, tok, width), F32),
            pltpu.VMEM((tok, width), BF16),
            pltpu.VMEM((n_step, prow, plane), BF16),
            pltpu.VMEM((n_step, prow, plane), BF16),
            pltpu.VMEM((tok, width), BF16),
            pltpu.VMEM((n_step, prow, plane), F32),
            pltpu.VMEM((tok, width), F32),
            dma((3,)), dma, dma((3,)), dma((3,)), dma((4,)), dma((4,)),
            dma((3,)), dma((3,)), dma((4,)), dma((4,)),
            dma, dma((7,)), dma((7,)),
            dma((n_step - 1,)), dma((n_step - 1,)), dma((n_step - 1,)), dma((n_step - 1,)),
        ],
        compiler_params=pltpu.CompilerParams(
            collective_id=0, has_side_effects=True, vmem_limit_bytes=50 * 1024 * 1024),
        name="picard",
    )(start_state, te, qkv_weight, out_weight)
    return start_state[None] + (1.0 / (2 * n_step)) * sums


def solution(mesh):
    return jax.shard_map(
        functools.partial(on_device, mesh.shape["step"]),
        mesh=mesh,
        in_specs=(P("seq", None), P("step"), P(), P("seq", None)),
        out_specs=P("step", "seq", None),
        check_vma=False,
    )
```

time: 475 us -> 160 us (0.34)
  the two profiles are of different devices: /device:TPU:103 before, /device:TPU:0 now
where the time goes in v1:
time: 160 us; the launch traced here: 159 us
  Pallas kernels  155 us (97%)
  local copies, waits for them, and re-layouts  2.26 us (1%)
  other arithmetic  2.15 us (1%)
    pallas_call x1, Pallas kernels, on_device(): pl.pallas_call(functools.partial(kernel, n_step), out_shape=jax.ShapeDtyp...  155 us

profile of v1, /device:TPU:0, one launch (start us, length us, event | category | flops | bytes accessed | tf_op | source)
XLA Modules:
  0.0 159.5 jit_solution(14251349309758289559)
XLA Ops:
  0.0 0.7 convert_element_type.3
  0.7 0.2 multiply_sine_fusion
  0.9 0.0 copy-start
  0.9 1.1 copy-done
  2.0 0.0 copy-start.1
  2.0 1.1 copy-done.1
  3.1 155.0 %picard.1 = f32[2,128,1536]{2,1,0:T(8,128)S(1)} custom-call(f32[128,1536]{1,0:T(8,128)S(1)} %copy-done, f32[2,1536]{1,0:T(2,128)S(1)} %pad_maximum_fusion.te_ref, bf16[1536,6144]{1,0:T(8,128)(2,1)} %wqkv_ref.1, bf16[256,1536]{1,0:T(8,128)(2,1)S(1)} %copy-done.1), custom_call_target="tpu_custom_call" | custom-call | tf_op jit(solution)/shard_map/picard/pallas_call | solution.py:331
  158.2 1.3 multiply_add_fusion
  (2 shorter events, 0.0 us)
Async XLA Ops:
  0.9 1.1 copy-start
  2.0 1.1 copy-start.1

commit v2 on v0

v2 whole, which is shorter than its diff:
```python
import functools
import math

import jax
import jax.numpy as jnp
from jax import lax
from jax.experimental import pallas as pl
from jax.experimental.pallas import tpu as pltpu
from jax.sharding import PartitionSpec as P

HEAD_SIZE = 128
HEADS = 16
INNER = HEADS * HEAD_SIZE
STEP_DEVS = 16
SEQ_DEVS = 8
STEPS = 32
NORM_EPS = 1e-06
MESH = pl.DeviceIdType.MESH
F32 = jnp.float32
BF16 = jnp.bfloat16
QUERY_SCALE = math.log2(math.e) / math.sqrt(HEAD_SIZE)


def embed(step_index, model_width):
    half_width = model_width // 2
    frequency = jnp.exp(-math.log(10000.0) * jnp.arange(half_width, dtype=F32) / half_width)
    angles = step_index.astype(F32)[:, None] * frequency[None, :]
    return jnp.concatenate([jnp.sin(angles), jnp.cos(angles)], axis=1)


def remote(src, dst, send_sem, recv_sem, device):
    return pltpu.make_async_remote_copy(
        src_ref=src, dst_ref=dst, send_sem=send_sem, recv_sem=recv_sem,
        device_id=device, device_id_type=MESH)


def aligned(value, by):
    return pl.multiple_of(value, by)


def each(first, last, body):
    def step(k, carry):
        body(k)
        return carry

    lax.fori_loop(first, last, step, 0)


def split_dot(values, weights):
    high = values.astype(BF16)
    low = (values - high.astype(F32)).astype(BF16)
    return (jnp.dot(high, weights, preferred_element_type=F32)
            + jnp.dot(low, weights, preferred_element_type=F32))


def softmax_mix(queries, keys, values):
    scores = lax.dot_general(queries, keys, (((1,), (1,)), ((), ())), preferred_element_type=F32)
    expo = jnp.exp2(scores - jnp.max(scores, axis=1, keepdims=True))
    total = jnp.sum(expo, axis=1, keepdims=True)
    mixed = jnp.dot(expo.astype(BF16), values, preferred_element_type=F32)
    return (mixed / total).astype(BF16)


def kernel(
    te_ref, start_ref, wqkv_ref, wout_ref,
    out_ref,
    w1, w2, wo, st, tea, tes, swb, rtb, tew, qkv1, att1, recv1, dr1, bs1, pr1, pe1, e1, stb, ns,
    xs, qkv2, att2, recv2, dr2, bs2, pr2, pe2, e2,
    w1_sem, w2_sem, wo_sem, st_sem,
    te_send, te_recv, sw_send, sw_recv, swf_send, swf_recv, rt_send, rt_recv, sb_send, sb_recv,
    wy_send, wy_recv, wz_send, wz_recv, wf_send, wf_recv,
    a1_send, a1_recv, p1_send, p1_recv, e1_send, e1_recv,
    x_send, x_recv, xf_send, xf_recv,
    a2_send, a2_recv, a2_sem, p2_send, p2_recv, e2_send, e2_recv,
):
    tok, width = start_ref.shape
    half, part = tok // 2, tok // 4
    lane4 = width // 4
    orow = wout_ref.shape[0]
    s = lax.axis_index("step")
    q = lax.axis_index("seq")
    y, c = q // 2, q % 2
    parity = y // 2
    group = (y % 2) * 2 + c
    gw = INNER // 4
    scale = 1.0 / STEPS
    here = (s, q)
    mate = (s, 2 * y + 1 - c)

    def chip(dy):
        return lax.rem(y + dy, 4)

    def step_peer(k):
        return lax.rem(s + k, STEP_DEVS)

    def seq_peer(k):
        return lax.rem(q + k, SEQ_DEVS)

    def w1_copy(n):
        return pltpu.make_async_copy(
            wqkv_ref.at[:, pl.ds(aligned(n * INNER + s * HEAD_SIZE, 128), HEAD_SIZE)],
            w1.at[:, pl.ds(n * HEAD_SIZE, HEAD_SIZE)], w1_sem.at[n])

    def w2_copy(n):
        return pltpu.make_async_copy(
            wqkv_ref.at[:, pl.ds(aligned(n * INNER + group * gw, 128), gw)],
            w2.at[:, pl.ds(n * gw, gw)], w2_sem.at[n])

    def st_copy(n):
        h, b = n // 2, n % 2
        return pltpu.make_async_copy(
            start_ref.at[pl.ds(half * b + part * h, part)],
            st.at[pl.ds(half * h + part * b, part)], st_sem.at[n])

    def wo_rows(owner, first, count):
        return wo.at[pl.ds(aligned(owner * orow + first, 16), count)]

    wo_own = pltpu.make_async_copy(wout_ref, wo_rows(q, 0, orow), wo_sem)
    for n in range(4):
        st_copy(n).start()
    for n in range(3):
        w1_copy(n).start()
    wo_own.start()

    barrier = pltpu.get_barrier_semaphore()
    for k in range(1, STEP_DEVS):
        pl.semaphore_signal(barrier, inc=1, device_id=(step_peer(k), q), device_id_type=MESH)
    for k in range(1, SEQ_DEVS):
        pl.semaphore_signal(barrier, inc=1, device_id=(s, seq_peer(k)), device_id_type=MESH)
    pl.semaphore_wait(barrier, STEP_DEVS - 1 + SEQ_DEVS - 1)

    def te_copy(k):
        return remote(te_ref, tea.at[s], te_send.at[k - 1], te_recv.at[k - 1], (step_peer(k), q))

    def te_arrival(k):
        return remote(te_ref, tea.at[step_peer(STEP_DEVS - k)], te_send.at[k - 1], te_recv.at[k - 1], here)

    each(1, STEP_DEVS, lambda k: te_copy(k).start())
    tea[s] = te_ref[...]

    for n in range(4):
        st_copy(n).wait()
    for n in range(3):
        w1_copy(n).wait()
    lane = lax.broadcasted_iota(jnp.int32, (1, 3 * HEAD_SIZE), 1)
    factor = jnp.where(lane < HEAD_SIZE, QUERY_SCALE, 1.0)
    swb[q] = (split_dot(st[...], w1[...]) * factor).astype(BF16)

    def sw_copy(dy):
        return remote(swb.at[q], swb.at[q], sw_send.at[dy - 1], sw_recv.at[dy - 1], (s, 2 * chip(dy) + c))

    def sw_arrival(dy):
        return remote(swb.at[q], swb.at[2 * chip(4 - dy) + c], sw_send.at[dy - 1], sw_recv.at[dy - 1], here)

    def sw_forward(dy):
        owner = 2 * chip(4 - dy) + c
        return remote(swb.at[owner], swb.at[owner], swf_send.at[dy % 4], swf_recv.at[dy % 4], mate)

    def sw_forwarded(dy):
        owner = 2 * chip(4 - dy) + 1 - c
        return remote(swb.at[owner], swb.at[owner], swf_send.at[dy % 4], swf_recv.at[dy % 4], mate)

    for dy in (2, 1, 3):
        sw_copy(dy).start()
    sw_forward(0).start()

    zp = (s // 4) % 2

    def wy_copy(dy):
        return remote(wout_ref.at[pl.ds(aligned(zp * (orow // 2), 16), orow // 2)],
                      wo_rows(q, zp * (orow // 2), orow // 2),
                      wy_send.at[dy - 1], wy_recv.at[dy - 1], (s, 2 * chip(dy) + c))

    def wy_arrival(dy):
        rows = wo_rows(2 * chip(4 - dy) + c, zp * (orow // 2), orow // 2)
        return remote(rows, rows, wy_send.at[dy - 1], wy_recv.at[dy - 1], here)

    def wz_copy(dy, up):
        rows = wo_rows(2 * chip(4 - dy) + c, zp * (orow // 2) + up * (orow // 4), orow // 4)
        return remote(rows, rows, wz_send.at[2 * dy - 2 + up], wz_recv.at[2 * dy - 2 + up],
                      (step_peer(4 if up else STEP_DEVS - 4), q))

    def wz_arrival(dy, up):
        rows = wo_rows(2 * chip(4 - dy) + c, (1 - zp) * (orow // 2) + up * (orow // 4), orow // 4)
        return remote(rows, rows, wz_send.at[2 * dy - 2 + up], wz_recv.at[2 * dy - 2 + up], here)

    def wf_rows(n, core):
        if n == 0:
            return wo_rows(2 * y + core, 0, orow)
        dy, kind = (n - 1) // 3 + 1, (n - 1) % 3
        owner = 2 * chip(4 - dy) + core
        if kind == 0:
            return wo_rows(owner, zp * (orow // 2), orow // 2)
        return wo_rows(owner, (1 - zp) * (orow // 2) + (kind - 1) * (orow // 4), orow // 4)

    def wf_copy(n):
        return remote(wf_rows(n, c), wf_rows(n, c), wf_send.at[n], wf_recv.at[n], mate)

    def wf_arrival(n):
        return remote(wf_rows(n, 1 - c), wf_rows(n, 1 - c), wf_send.at[n], wf_recv.at[n], mate)

    for dy in (2, 1, 3):
        wy_copy(dy).start()

    owner_q = s // 2
    block = s % 2

    def sb_src(h):
        return st.at[pl.ds(aligned(half * h + part * block, 8), part)]

    def sb_copy(k, h):
        return remote(sb_src(h), stb.at[h], sb_send.at[h, k - 1], sb_recv.at[h], (s, seq_peer(k)))

    @pl.when(q == owner_q)
    def _():
        for h in range(2):
            each(1, SEQ_DEVS, lambda k: sb_copy(k, h).start())
            stb[h] = sb_src(h)[...]

    for n in range(3):
        w2_copy(n).start()

    each(1, STEP_DEVS, lambda k: te_arrival(k).wait_recv())
    for n in range(STEP_DEVS):
        tes[2 * n:2 * n + 2, :] = tea[n]
    own = st[...]
    cross = lax.dot_general(tes[...], own, (((1,), (1,)), ((), ())),
                            precision=lax.Precision.HIGHEST, preferred_element_type=F32)
    squares = lax.dot_general(jnp.ones((8, width), F32), own * own, (((1,), (1,)), ((), ())),
                              precision=lax.Precision.HIGHEST, preferred_element_type=F32)[0:1]
    step_squares = jnp.sum(tes[...] * tes[...], axis=1, keepdims=True)
    mean_square = jnp.maximum((squares + 2.0 * cross + step_squares) * (1.0 / width), 0.0)
    rtb[q] = lax.rsqrt(mean_square + NORM_EPS)

    def rt_copy(k):
        return remote(rtb.at[q], rtb.at[q], rt_send.at[k - 1], rt_recv.at[k - 1], (s, seq_peer(k)))

    def rt_arrival(k):
        return remote(rtb.at[q], rtb.at[seq_peer(SEQ_DEVS - k)], rt_send.at[k - 1], rt_recv.at[k - 1], here)

    each(1, SEQ_DEVS, lambda k: rt_copy(k).start())
    tew[...] = split_dot(tes[...], w1[...]) * factor

    for dy in (1, 3, 2):
        sw_arrival(dy).wait_recv()
        sw_forward(dy).start()
    each(1, SEQ_DEVS, lambda k: rt_arrival(k).wait_recv())
    for dy in range(4):
        sw_forwarded(dy).wait_recv()

    def build(n):
        i, b = n // SEQ_DEVS, lax.rem(n, SEQ_DEVS)
        k = 4 * q + i
        pick = (lax.broadcasted_iota(jnp.int32, (STEPS, HEAD_SIZE), 0) == k).astype(F32)
        rows = lax.dot_general(rtb[b], pick, (((0,), (0,)), ((), ())),
                               precision=lax.Precision.HIGHEST, preferred_element_type=F32)
        step_row = tew[pl.ds(k, 1), :]
        for n3 in range(3):
            cols = slice(n3 * HEAD_SIZE, (n3 + 1) * HEAD_SIZE)
            qkv1[i, b, :, cols] = ((swb[b, :, cols].astype(F32) + step_row[:, cols]) * rows).astype(BF16)

    each(0, 4 * SEQ_DEVS, build)

    def a1_copy(h, k):
        return remote(att1.at[h, step_peer(k)], recv1.at[h, :, pl.ds(aligned(s * HEAD_SIZE, 128), HEAD_SIZE)],
                      a1_send.at[h, k - 1], a1_recv.at[h, k - 1], (step_peer(k), q))

    def a1_arrival(h, k):
        src = step_peer(STEP_DEVS - k)
        return remote(att1.at[h, s], recv1.at[h, :, pl.ds(aligned(src * HEAD_SIZE, 128), HEAD_SIZE)],
                      a1_send.at[h, k - 1], a1_recv.at[h, k - 1], here)

    for h in range(2):
        def attend1(n):
            i, sub = n // 2, lax.rem(n, 2)
            queries = qkv1[i, pl.ds(4 * sub, 4), half * h:half * (h + 1), 0:HEAD_SIZE].reshape(4 * half, HEAD_SIZE)
            keys = qkv1[i, :, :, HEAD_SIZE:2 * HEAD_SIZE].reshape(8 * tok, HEAD_SIZE)
            values = qkv1[i, :, :, 2 * HEAD_SIZE:3 * HEAD_SIZE].reshape(8 * tok, HEAD_SIZE)
            mixed = softmax_mix(queries, keys, values).reshape(8, part, HEAD_SIZE)
            att1[h, pl.ds(8 * sub, 8), pl.ds(aligned(i * part, part), part), :] = mixed

        each(0, 8, attend1)
        each(1, STEP_DEVS, lambda k: a1_copy(h, k).start())
        recv1[h, :, pl.ds(aligned(s * HEAD_SIZE, 128), HEAD_SIZE)] = att1[h, s]
        if h == 0:
            wo_own.wait()
            wf_copy(0).start()
            for dy in (1, 3, 2):
                wy_arrival(dy).wait_recv()
                wz_copy(dy, 0).start()
                wz_copy(dy, 1).start()
                wf_copy(3 * dy - 2).start()
        else:
            for dy in (1, 3, 2):
                for up in range(2):
                    wz_arrival(dy, up).wait_recv()
                    wf_copy(3 * dy - 1 + up).start()
    for n in range(10):
        wf_arrival(n).wait_recv()

    def piece(ref, who):
        return ref.at[pl.ds(aligned((who // 4) * 16, 16), 16), pl.ds(aligned((who % 4) * lane4, 128), lane4)]

    def p1_copy(h, k):
        dest = seq_peer(k)
        return remote(piece(bs1.at[h], dest), pr1.at[h, q], p1_send.at[h, k - 1], p1_recv.at[h, k - 1], (s, dest))

    def p1_arrival(h, k):
        return remote(piece(bs1.at[h], q), pr1.at[h, seq_peer(SEQ_DEVS - k)],
                      p1_send.at[h, k - 1], p1_recv.at[h, k - 1], here)

    def e1_copy(h, k):
        dest = seq_peer(k)
        return remote(pe1.at[h, dest], piece(e1.at[h], q), e1_send.at[h, k - 1], e1_recv.at[h, k - 1], (s, dest))

    def e1_arrival(h, k):
        return remote(pe1.at[h, q], piece(e1.at[h], seq_peer(SEQ_DEVS - k)),
                      e1_send.at[h, k - 1], e1_recv.at[h, k - 1], here)

    def drift1(h):
        each(1, STEP_DEVS, lambda k: a1_arrival(h, k).wait_recv())

        def tile(n):
            cols = pl.ds(aligned(n * 256, 256), 256)
            rows = jnp.dot(recv1[h], wo[:, cols], preferred_element_type=F32)
            total = rows[0:part]
            dr1[h, 0, :, cols] = total
            for i in range(1, 4):
                total = total + rows[i * part:(i + 1) * part]
                dr1[h, i, :, cols] = total
            bs1[h, :, cols] = total.astype(BF16)

        each(0, width // 256, tile)
        each(1, SEQ_DEVS, lambda k: p1_copy(h, k).start())
        pr1[h, q] = piece(bs1.at[h], q)[...]

    def scan1(h):
        each(1, SEQ_DEVS, lambda k: p1_arrival(h, k).wait_recv())
        total = jnp.zeros((16, lane4), F32)
        for k in range(SEQ_DEVS):
            pe1[h, k] = total.astype(BF16)
            total = total + pr1[h, k].astype(F32)
        each(1, SEQ_DEVS, lambda k: e1_copy(h, k).start())
        piece(e1.at[h], q)[...] = pe1[h, q]

    def x_rows(h, who):
        return xs.at[pl.ds(aligned(h * 8 * half + who * part, part), part)]

    def x_target(h, n):
        i, e = n // 2, n % 2
        return 2 * q + i // 2, 2 * (2 * (i % 2) + e) + lax.rem(s + h, 2)

    def x_copy(h, n):
        return remote(ns.at[h, n // 2], x_rows(h, s), x_send.at[h, n], x_recv.at[h, s // 2], x_target(h, n))

    def is_here(h, n):
        a, b = x_target(h, n)
        return jnp.logical_and(a == s, b == q)

    def x_local(h, n):
        return pltpu.make_async_copy(ns.at[h, n // 2], x_rows(h, s), x_recv.at[h, s // 2])

    def direct(h, m):
        return 2 * m + lax.rem(c + h, 2)

    def x_arrival(h, m):
        rows = x_rows(h, direct(h, m))
        return pltpu.make_async_copy(rows, rows, x_recv.at[h, m])

    def x_forward(h, m):
        rows = x_rows(h, direct(h, m))
        return remote(rows, rows, xf_send.at[h, m], xf_recv.at[h, m], mate)

    def x_forwarded(h, m):
        rows = x_rows(h, 2 * m + lax.rem(c + h + 1, 2))
        return remote(rows, rows, xf_send.at[h, m], xf_recv.at[h, m], mate)

    def states(h):
        each(1, SEQ_DEVS, lambda k: e1_arrival(h, k).wait_recv())
        for i in range(4):
            before = e1[h].astype(F32)
            if i:
                before = before + dr1[h, i - 1]
            shifted = stb[h] + scale * before + tes[pl.ds(4 * q + i, 1), :]
            mean = jnp.mean(shifted * shifted, axis=1, keepdims=True)
            ns[h, i] = (shifted * lax.rsqrt(mean + NORM_EPS)).astype(BF16)
            for n in (2 * i, 2 * i + 1):
                @pl.when(is_here(h, n))
                def _():
                    x_local(h, n).start()

                @pl.when(jnp.logical_not(is_here(h, n)))
                def _():
                    x_copy(h, n).start()

    @pl.when(q != owner_q)
    def _():
        for h in range(2):
            sb_copy_in = remote(stb.at[h], stb.at[h], sb_send.at[h, 0], sb_recv.at[h], here)
            sb_copy_in.wait_recv()

    drift1(0)
    scan1(0)
    drift1(1)
    states(0)
    scan1(1)
    states(1)

    for n in range(3):
        w2_copy(n).wait()

    def project(h, sub):
        rows = pl.ds(h * 8 * half + sub * 4 * half, 4 * half)

        def columns(n):
            cols = pl.ds(aligned(n * gw, gw), gw)
            f = jnp.where(n == 0, QUERY_SCALE, 1.0)
            qkv2[rows, cols] = (jnp.dot(xs[rows, :], w2[:, cols], preferred_element_type=F32) * f).astype(BF16)

        each(0, 3, columns)

    for h in range(2):
        for sub in range(2):
            for m in range(4 * sub, 4 * sub + 4):
                x_arrival(h, m).wait()
                x_forward(h, m).start()
        for sub in range(2):
            for m in range(4 * sub, 4 * sub + 4):
                x_forwarded(h, m).wait_recv()
            project(h, sub)

    def a2_block(h, who):
        yy, cc = who // 2, who % 2
        return recv2.at[h, pl.ds(aligned((yy // 2) * half, half), half),
                        pl.ds(aligned(((yy % 2) * 2 + cc) * gw, gw), gw)]

    def att2_rows(h, who):
        return att2.at[pl.ds(aligned(h * 8 * half + who * half, half), half)]

    def a2_copy(h, k):
        dest = seq_peer(k)
        return remote(att2_rows(h, dest), a2_block(h, q), a2_send.at[h, k - 1], a2_recv.at[h, k - 1], (s, dest))

    def a2_arrival(h, k):
        return remote(att2_rows(h, q), a2_block(h, seq_peer(SEQ_DEVS - k)),
                      a2_send.at[h, k - 1], a2_recv.at[h, k - 1], here)

    def a2_own(h):
        return pltpu.make_async_copy(att2_rows(h, q), a2_block(h, q), a2_sem.at[h])

    for h in range(2):
        def attend2(n):
            sub, head = n // 4, lax.rem(n, 4)
            rows = pl.ds(aligned(h * 8 * half + sub * 4 * half, 4 * half), 4 * half)

            def cols(p):
                return pl.ds(aligned(p * gw + head * HEAD_SIZE, HEAD_SIZE), HEAD_SIZE)

            att2[rows, cols(0)] = softmax_mix(qkv2[rows, cols(0)], qkv2[:, cols(1)], qkv2[:, cols(2)])

        each(0, 8, attend2)
        each(1, SEQ_DEVS, lambda k: a2_copy(h, k).start())
        a2_own(h).start()

    def p2_copy(h, k):
        dest = step_peer(k)
        return remote(piece(bs2.at[h], dest), pr2.at[h, s], p2_send.at[h, k - 1], p2_recv.at[h, k - 1], (dest, q))

    def p2_arrival(h, k):
        return remote(piece(bs2.at[h], s), pr2.at[h, step_peer(STEP_DEVS - k)],
                      p2_send.at[h, k - 1], p2_recv.at[h, k - 1], here)

    def e2_copy(h, k):
        dest = step_peer(k)
        return remote(pe2.at[h, dest], piece(e2.at[h], s), e2_send.at[h, k - 1], e2_recv.at[h, k - 1], (dest, q))

    def e2_arrival(h, k):
        return remote(pe2.at[h, s], piece(e2.at[h], step_peer(STEP_DEVS - k)),
                      e2_send.at[h, k - 1], e2_recv.at[h, k - 1], here)

    def drift2(h):
        a2_own(h).wait()
        each(1, SEQ_DEVS, lambda k: a2_arrival(h, k).wait_recv())

        def tile(n):
            cols = pl.ds(aligned(n * 256, 256), 256)
            rows = jnp.dot(recv2[h], wo[:, cols], preferred_element_type=F32)
            first = rows[0:half]
            total = first + rows[half:]
            dr2[h, 0, :, cols] = first
            dr2[h, 1, :, cols] = total
            bs2[h, :, cols] = total.astype(BF16)

        each(0, width // 256, tile)
        each(1, STEP_DEVS, lambda k: p2_copy(h, k).start())
        pr2[h, s] = piece(bs2.at[h], s)[...]

    def scan2(h):
        each(1, STEP_DEVS, lambda k: p2_arrival(h, k).wait_recv())
        total = jnp.zeros((16, lane4), F32)
        for k in range(STEP_DEVS):
            pe2[h, k] = total
            total = total + pr2[h, k].astype(F32)
        each(1, STEP_DEVS, lambda k: e2_copy(h, k).start())
        piece(e2.at[h], s)[...] = pe2[h, s]

    def finish(h):
        each(1, STEP_DEVS, lambda k: e2_arrival(h, k).wait_recv())
        for i in range(2):
            for b in range(2):
                rows = slice(part * b, part * (b + 1))
                out_ref[i, half * b + part * h:half * b + part * (h + 1), :] = e2[h, rows, :] + dr2[h, i, rows, :]

    drift2(0)
    scan2(0)
    drift2(1)
    scan2(1)
    finish(0)
    finish(1)

    each(1, STEP_DEVS, lambda k: te_copy(k).wait_send())
    for dy in range(1, 4):
        sw_copy(dy).wait_send()
        wy_copy(dy).wait_send()
        for up in range(2):
            wz_copy(dy, up).wait_send()
    for dy in range(4):
        sw_forward(dy).wait_send()
    for n in range(10):
        wf_copy(n).wait_send()
    each(1, SEQ_DEVS, lambda k: rt_copy(k).wait_send())

    @pl.when(q == owner_q)
    def _():
        for h in range(2):
            each(1, SEQ_DEVS, lambda k: sb_copy(k, h).wait_send())

    for h in range(2):
        for k in range(1, SEQ_DEVS):
            p1_copy(h, k).wait_send()
            e1_copy(h, k).wait_send()
            a2_copy(h, k).wait_send()
        for k in range(1, STEP_DEVS):
            a1_copy(h, k).wait_send()
            p2_copy(h, k).wait_send()
            e2_copy(h, k).wait_send()
        for n in range(8):
            @pl.when(jnp.logical_not(is_here(h, n)))
            def _():
                x_copy(h, n).wait_send()
        for m in range(8):
            x_forward(h, m).wait_send()


def on_device(start_state, timesteps, qkv_weight, out_weight):
    tok, width = start_state.shape
    half, part, lane4 = tok // 2, tok // 4, width // 4
    te = embed(timesteps, width)
    dma = pltpu.SemaphoreType.DMA
    vmem = pl.BlockSpec(memory_space=pltpu.VMEM)
    hbm = pl.BlockSpec(memory_space=pl.ANY)
    sums = pl.pallas_call(
        kernel,
        out_shape=jax.ShapeDtypeStruct((2, tok, width), F32),
        in_specs=[vmem, hbm, hbm, hbm],
        out_specs=vmem,
        scratch_shapes=[
            pltpu.VMEM((width, 3 * HEAD_SIZE), BF16),
            pltpu.VMEM((width, 3 * INNER // 4), BF16),
            pltpu.VMEM((INNER, width), BF16),
            pltpu.VMEM((tok, width), F32),
            pltpu.VMEM((STEP_DEVS, 2, width), F32),
            pltpu.VMEM((STEPS, width), F32),
            pltpu.VMEM((SEQ_DEVS, tok, 3 * HEAD_SIZE), BF16),
            pltpu.VMEM((SEQ_DEVS, STEPS, tok), F32),
            pltpu.VMEM((STEPS, 3 * HEAD_SIZE), F32),
            pltpu.VMEM((4, SEQ_DEVS, tok, 3 * HEAD_SIZE), BF16),
            pltpu.VMEM((2, STEP_DEVS, 4 * part, HEAD_SIZE), BF16),
            pltpu.VMEM((2, 4 * part, INNER), BF16),
            pltpu.VMEM((2, 4, part, width), F32),
            pltpu.VMEM((2, part, width), BF16),
            pltpu.VMEM((2, SEQ_DEVS, 16, lane4), BF16),
            pltpu.VMEM((2, SEQ_DEVS, 16, lane4), BF16),
            pltpu.VMEM((2, part, width), BF16),
            pltpu.VMEM((2, part, width), F32),
            pltpu.VMEM((2, 4, part, width), BF16),
            pltpu.VMEM((8 * tok, width), BF16),
            pltpu.VMEM((8 * tok, 3 * INNER // 4), BF16),
            pltpu.VMEM((8 * tok, INNER // 4), BF16),
            pltpu.VMEM((2, tok, INNER), BF16),
            pltpu.VMEM((2, 2, half, width), F32),
            pltpu.VMEM((2, half, width), BF16),
            pltpu.VMEM((2, STEP_DEVS, 16, lane4), BF16),
            pltpu.VMEM((2, STEP_DEVS, 16, lane4), F32),
            pltpu.VMEM((2, half, width), F32),
            dma((3,)), dma((3,)), dma, dma((4,)),
            dma((15,)), dma((15,)), dma((3,)), dma((3,)), dma((4,)), dma((4,)), dma((7,)), dma((7,)),
            dma((2, 7)), dma((2,)),
            dma((3,)), dma((3,)), dma((6,)), dma((6,)), dma((10,)), dma((10,)),
            dma((2, 15)), dma((2, 15)), dma((2, 7)), dma((2, 7)), dma((2, 7)), dma((2, 7)),
            dma((2, 8)), dma((2, 8)), dma((2, 8)), dma((2, 8)),
            dma((2, 7)), dma((2, 7)), dma((2,)), dma((2, 15)), dma((2, 15)), dma((2, 15)), dma((2, 15)),
        ],
        compiler_params=pltpu.CompilerParams(
            collective_id=0, has_side_effects=True, vmem_limit_bytes=58 * 1024 * 1024),
        name="picard",
    )(te, start_state, qkv_weight, out_weight)
    return start_state[None] + (1.0 / STEPS) * sums


def solution(mesh):
    return jax.shard_map(
        on_device,
        mesh=mesh,
        in_specs=(P("seq", None), P("step"), P(), P("seq", None)),
        out_specs=P("step", "seq", None),
        check_vma=False,
    )
```

time: 475 us -> 185 us (0.39)
  the two profiles are of different devices: /device:TPU:103 before, /device:TPU:0 now
where the time goes in v2:
time: 185 us
  Pallas kernels  181 us (98%)
  other arithmetic  4.16 us (2%)
    pallas_call x1, Pallas kernels, on_device(): pl.pallas_call(kernel, out_shape=jax.ShapeDtypeStruct((2, tok, width), F3...  181 us

profile of v2, /device:TPU:0, one launch (start us, length us, event | category | flops | bytes accessed | tf_op | source)
XLA Modules:
  0.0 185.1 jit_solution(13020994237993607276)
XLA Ops:
  0.0 0.7 convert_element_type.3
  0.7 0.2 multiply_sine_fusion
  0.8 0.6 pad_maximum_fusion.te_ref
  1.5 0.0 copy-start
  1.5 180.9 %picard.1 = f32[2,128,1536]{2,1,0:T(8,128)} custom-call(f32[2,1536]{1,0:T(2,128)} %pad_maximum_fusion.te_ref, f32[128,1536]{1,0:T(8,128)} %start_ref.1, bf16[1536,6144]{1,0:T(8,128)(2,1)} %wqkv_ref.1, bf16[256,1536]{1,0:T(8,128)(2,1)} %wout_ref.1), custom_call_target="tpu_custom_call" | custom-call | tf_op jit(solution)/shard_map/picard/pallas_call | solution.py:562
  182.4 0.0 copy-done
  182.4 2.7 %multiply_add_fusion = f32[2,128,1536]{2,1,0:T(8,128)} fusion(f32[2,128,1536]{2,1,0:T(8,128)} %picard.1, f32[128,1536]{1,0:T(8,128)S(1)} %copy-done), kind=kLoop, calls=%fused_computation | loop fusion | flops 786432 | bytes 3932160 | tf_op jit(solution)/shard_map/add | solution.py:608
  (1 shorter events, 0.0 us)
Async XLA Ops:
  1.5 180.9 %copy-start = (f32[128,1536]{1,0:T(8,128)S(1)}, f32[128,1536]{1,0:T(8,128)}, u32[]{:S(2)}) copy-start(f32[128,1536]{1,0:T(8,128)} %start_ref.1) | copy-start | bytes 2359300

commit v3 on v2

--- a/solution.py
+++ b/solution.py
@@ -68,7 +68,7 @@
     xs, qkv2, att2, recv2, dr2, bs2, pr2, pe2, e2,
     w1_sem, w2_sem, wo_sem, st_sem,
     te_send, te_recv, sw_send, sw_recv, swf_send, swf_recv, rt_send, rt_recv, sb_send, sb_recv,
-    wy_send, wy_recv, wz_send, wz_recv, wf_send, wf_recv,
+    wy_send, wy_recv, wr_send, wr_recv, wn_send, wn_recv, wf_send, wf_recv,
     a1_send, a1_recv, p1_send, p1_recv, e1_send, e1_recv,
     x_send, x_recv, xf_send, xf_recv,
     a2_send, a2_recv, a2_sem, p2_send, p2_recv, e2_send, e2_recv,
@@ -123,20 +123,10 @@
     wo_own.start()
 
     barrier = pltpu.get_barrier_semaphore()
-    for k in range(1, STEP_DEVS):
-        pl.semaphore_signal(barrier, inc=1, device_id=(step_peer(k), q), device_id_type=MESH)
-    for k in range(1, SEQ_DEVS):
-        pl.semaphore_signal(barrier, inc=1, device_id=(s, seq_peer(k)), device_id_type=MESH)
-    pl.semaphore_wait(barrier, STEP_DEVS - 1 + SEQ_DEVS - 1)
-
-    def te_copy(k):
-        return remote(te_ref, tea.at[s], te_send.at[k - 1], te_recv.at[k - 1], (step_peer(k), q))
-
-    def te_arrival(k):
-        return remote(te_ref, tea.at[step_peer(STEP_DEVS - k)], te_send.at[k - 1], te_recv.at[k - 1], here)
-
-    each(1, STEP_DEVS, lambda k: te_copy(k).start())
-    tea[s] = te_ref[...]
+    each(1, STEP_DEVS, lambda k: pl.semaphore_signal(
+        barrier, inc=1, device_id=(step_peer(k), q), device_id_type=MESH))
+    each(1, SEQ_DEVS, lambda k: pl.semaphore_signal(
+        barrier, inc=1, device_id=(s, seq_peer(k)), device_id_type=MESH))
 
     for n in range(4):
         st_copy(n).wait()
@@ -145,6 +135,16 @@
     lane = lax.broadcasted_iota(jnp.int32, (1, 3 * HEAD_SIZE), 1)
     factor = jnp.where(lane < HEAD_SIZE, QUERY_SCALE, 1.0)
     swb[q] = (split_dot(st[...], w1[...]) * factor).astype(BF16)
+    pl.semaphore_wait(barrier, STEP_DEVS - 1 + SEQ_DEVS - 1)
+
+    def te_copy(k):
+        return remote(te_ref, tea.at[s], te_send.at[k - 1], te_recv.at[k - 1], (step_peer(k), q))
+
+    def te_arrival(k):
+        return remote(te_ref, tea.at[step_peer(STEP_DEVS - k)], te_send.at[k - 1], te_recv.at[k - 1], here)
+
+    each(1, STEP_DEVS, lambda k: te_copy(k).start())
+    tea[s] = te_ref[...]
 
     def sw_copy(dy):
         return remote(swb.at[q], swb.at[q], sw_send.at[dy - 1], sw_recv.at[dy - 1], (s, 2 * chip(dy) + c))
@@ -164,34 +164,49 @@
         sw_copy(dy).start()
     sw_forward(0).start()
 
-    zp = (s // 4) % 2
+    zx = (s // 4 + s) % 2
+    hrow, qrow, erow = orow // 2, orow // 4, orow // 8
+
+    def wo_of(n, core, first, count):
+        return wo_rows(2 * chip(n) + core, first, count)
 
     def wy_copy(dy):
-        return remote(wout_ref.at[pl.ds(aligned(zp * (orow // 2), 16), orow // 2)],
-                      wo_rows(q, zp * (orow // 2), orow // 2),
+        return remote(wout_ref.at[pl.ds(aligned(zx * hrow, 16), hrow)], wo_rows(q, zx * hrow, hrow),
                       wy_send.at[dy - 1], wy_recv.at[dy - 1], (s, 2 * chip(dy) + c))
 
     def wy_arrival(dy):
-        rows = wo_rows(2 * chip(4 - dy) + c, zp * (orow // 2), orow // 2)
+        rows = wo_of(4 - dy, c, zx * hrow, hrow)
         return remote(rows, rows, wy_send.at[dy - 1], wy_recv.at[dy - 1], here)
 
-    def wz_copy(dy, up):
-        rows = wo_rows(2 * chip(4 - dy) + c, zp * (orow // 2) + up * (orow // 4), orow // 4)
-        return remote(rows, rows, wz_send.at[2 * dy - 2 + up], wz_recv.at[2 * dy - 2 + up],
-                      (step_peer(4 if up else STEP_DEVS - 4), q))
-
-    def wz_arrival(dy, up):
-        rows = wo_rows(2 * chip(4 - dy) + c, (1 - zp) * (orow // 2) + up * (orow // 4), orow // 4)
-        return remote(rows, rows, wz_send.at[2 * dy - 2 + up], wz_recv.at[2 * dy - 2 + up], here)
+    def wr_copy(r):
+        rows = wo_of(1 if r else 3, c, zx * hrow + r * qrow, qrow)
+        return remote(rows, rows, wr_send.at[r], wr_recv.at[r], (s, 2 * chip(3 if r else 1) + c))
+
+    def wr_arrival(r):
+        rows = wo_of(2, c, zx * hrow + r * qrow, qrow)
+        return remote(rows, rows, wr_send.at[r], wr_recv.at[r], here)
+
+    def neighbour(n):
+        if n < 2:
+            return step_peer(4 if n == 0 else STEP_DEVS - 4)
+        return (s // 4) * 4 + lax.rem(s + (1 if n == 2 else 3), 4)
+
+    def wn_copy(b, n):
+        rows = wo_of(b, c, zx * hrow + n * erow, erow)
+        return remote(rows, rows, wn_send.at[b - 1, n], wn_recv.at[b - 1, n], (neighbour(n), q))
+
+    def wn_arrival(b, n):
+        rows = wo_of(b, c, (1 - zx) * hrow + n * erow, erow)
+        return remote(rows, rows, wn_send.at[b - 1, n], wn_recv.at[b - 1, n], here)
 
     def wf_rows(n, core):
         if n == 0:
             return wo_rows(2 * y + core, 0, orow)
-        dy, kind = (n - 1) // 3 + 1, (n - 1) % 3
-        owner = 2 * chip(4 - dy) + core
-        if kind == 0:
-            return wo_rows(owner, zp * (orow // 2), orow // 2)
-        return wo_rows(owner, (1 - zp) * (orow // 2) + (kind - 1) * (orow // 4), orow // 4)
+        if n < 3:
+            return wo_of(1 if n == 1 else 3, core, zx * hrow, hrow)
+        if n < 5:
+            return wo_of(2, core, zx * hrow + (n - 3) * qrow, qrow)
+        return wo_of(n - 4, core, (1 - zx) * hrow, hrow)
 
     def wf_copy(n):
         return remote(wf_rows(n, c), wf_rows(n, c), wf_send.at[n], wf_recv.at[n], mate)
@@ -199,23 +214,50 @@
     def wf_arrival(n):
         return remote(wf_rows(n, 1 - c), wf_rows(n, 1 - c), wf_send.at[n], wf_recv.at[n], mate)
 
-    for dy in (2, 1, 3):
+    def wo_first():
+        for dy in (1, 3):
+            wy_arrival(dy).wait_recv()
+            wr_copy(0 if dy == 1 else 1).start()
+            for n in range(4):
+                wn_copy(4 - dy, n).start()
+            wf_copy(2 if dy == 1 else 1).start()
+
+    def wo_second():
+        for r in range(2):
+            wr_arrival(r).wait_recv()
+            wn_copy(2, 2 * r).start()
+            wn_copy(2, 2 * r + 1).start()
+            wf_copy(3 + r).start()
+        for b in (3, 1):
+            for n in range(4):
+                wn_arrival(b, n).wait_recv()
+            wf_copy(4 + b).start()
+
+    def wo_third():
+        for n in range(4):
+            wn_arrival(2, n).wait_recv()
+        wf_copy(6).start()
+        for n in range(8):
+            wf_arrival(n).wait_recv()
+
+    for dy in (1, 3):
         wy_copy(dy).start()
 
     owner_q = s // 2
     block = s % 2
 
-    def sb_src(h):
-        return st.at[pl.ds(aligned(half * h + part * block, 8), part)]
+    def sb_src(h, who):
+        return st.at[pl.ds(aligned(half * h + part * block + (who // 4) * 16, 8), 16),
+                     pl.ds(aligned((who % 4) * lane4, 128), lane4)]
 
     def sb_copy(k, h):
-        return remote(sb_src(h), stb.at[h], sb_send.at[h, k - 1], sb_recv.at[h], (s, seq_peer(k)))
+        return remote(sb_src(h, seq_peer(k)), stb.at[h], sb_send.at[h, k - 1], sb_recv.at[h], (s, seq_peer(k)))
 
     @pl.when(q == owner_q)
     def _():
         for h in range(2):
             each(1, SEQ_DEVS, lambda k: sb_copy(k, h).start())
-            stb[h] = sb_src(h)[...]
+            stb[h] = sb_src(h, q)[...]
 
     for n in range(3):
         w2_copy(n).start()
@@ -224,10 +266,19 @@
     for n in range(STEP_DEVS):
         tes[2 * n:2 * n + 2, :] = tea[n]
     own = st[...]
-    cross = lax.dot_general(tes[...], own, (((1,), (1,)), ((), ())),
-                            precision=lax.Precision.HIGHEST, preferred_element_type=F32)
-    squares = lax.dot_general(jnp.ones((8, width), F32), own * own, (((1,), (1,)), ((), ())),
-                              precision=lax.Precision.HIGHEST, preferred_element_type=F32)[0:1]
+    transposed = (((1,), (1,)), ((), ()))
+
+    def parts(values):
+        high = values.astype(BF16)
+        return high, (values - high.astype(F32)).astype(BF16)
+
+    def dot_t(a, b):
+        return lax.dot_general(a, b, transposed, preferred_element_type=F32)
+
+    own_parts, te_parts, square_parts = parts(own), parts(tes[...]), parts(own * own)
+    cross = dot_t(te_parts[0], own_parts[0]) + dot_t(te_parts[1], own_parts[0]) + dot_t(te_parts[0], own_parts[1])
+    one_row = jnp.ones((16, width), BF16)
+    squares = (dot_t(one_row, square_parts[0]) + dot_t(one_row, square_parts[1]))[0:1]
     step_squares = jnp.sum(tes[...] * tes[...], axis=1, keepdims=True)
     mean_square = jnp.maximum((squares + 2.0 * cross + step_squares) * (1.0 / width), 0.0)
     rtb[q] = lax.rsqrt(mean_square + NORM_EPS)
@@ -248,18 +299,22 @@
     for dy in range(4):
         sw_forwarded(dy).wait_recv()
 
-    def build(n):
-        i, b = n // SEQ_DEVS, lax.rem(n, SEQ_DEVS)
-        k = 4 * q + i
-        pick = (lax.broadcasted_iota(jnp.int32, (STEPS, HEAD_SIZE), 0) == k).astype(F32)
-        rows = lax.dot_general(rtb[b], pick, (((0,), (0,)), ((), ())),
-                               precision=lax.Precision.HIGHEST, preferred_element_type=F32)
-        step_row = tew[pl.ds(k, 1), :]
-        for n3 in range(3):
-            cols = slice(n3 * HEAD_SIZE, (n3 + 1) * HEAD_SIZE)
-            qkv1[i, b, :, cols] = ((swb[b, :, cols].astype(F32) + step_row[:, cols]) * rows).astype(BF16)
-
-    each(0, 4 * SEQ_DEVS, build)
+    pick_row = lax.broadcasted_iota(jnp.int32, (STEPS, 4 * HEAD_SIZE), 0)
+    pick_lane = lax.broadcasted_iota(jnp.int32, (STEPS, 4 * HEAD_SIZE), 1)
+    pick = (pick_row == 4 * q + pick_lane // HEAD_SIZE).astype(BF16)
+
+    def build(b):
+        scales = sum(lax.dot_general(rows, pick, (((0,), (0,)), ((), ())), preferred_element_type=F32)
+                     for rows in parts(rtb[b]))
+        base = swb[b].astype(F32)
+        for i in range(4):
+            rows = scales[:, i * HEAD_SIZE:(i + 1) * HEAD_SIZE]
+            step_row = tew[pl.ds(4 * q + i, 1), :]
+            for n3 in range(3):
+                cols = slice(n3 * HEAD_SIZE, (n3 + 1) * HEAD_SIZE)
+                qkv1[i, b, :, cols] = ((base[:, cols] + step_row[:, cols]) * rows).astype(BF16)
+
+    each(0, SEQ_DEVS, build)
 
     def a1_copy(h, k):
         return remote(att1.at[h, step_peer(k)], recv1.at[h, :, pl.ds(aligned(s * HEAD_SIZE, 128), HEAD_SIZE)],
@@ -271,32 +326,24 @@
                       a1_send.at[h, k - 1], a1_recv.at[h, k - 1], here)
 
     for h in range(2):
-        def attend1(n):
-            i, sub = n // 2, lax.rem(n, 2)
-            queries = qkv1[i, pl.ds(4 * sub, 4), half * h:half * (h + 1), 0:HEAD_SIZE].reshape(4 * half, HEAD_SIZE)
+        def attend1(i):
             keys = qkv1[i, :, :, HEAD_SIZE:2 * HEAD_SIZE].reshape(8 * tok, HEAD_SIZE)
             values = qkv1[i, :, :, 2 * HEAD_SIZE:3 * HEAD_SIZE].reshape(8 * tok, HEAD_SIZE)
-            mixed = softmax_mix(queries, keys, values).reshape(8, part, HEAD_SIZE)
-            att1[h, pl.ds(8 * sub, 8), pl.ds(aligned(i * part, part), part), :] = mixed
-
-        each(0, 8, attend1)
+            mixed = [softmax_mix(qkv1[i, 4 * sub:4 * sub + 4, half * h:half * (h + 1), 0:HEAD_SIZE].reshape(
+                4 * half, HEAD_SIZE), keys, values) for sub in range(2)]
+            for sub in range(2):
+                att1[h, 8 * sub:8 * sub + 8, pl.ds(aligned(i * part, part), part), :] = mixed[sub].reshape(
+                    8, part, HEAD_SIZE)
+
+        each(0, 4, attend1)
         each(1, STEP_DEVS, lambda k: a1_copy(h, k).start())
         recv1[h, :, pl.ds(aligned(s * HEAD_SIZE, 128), HEAD_SIZE)] = att1[h, s]
         if h == 0:
             wo_own.wait()
             wf_copy(0).start()
-            for dy in (1, 3, 2):
-                wy_arrival(dy).wait_recv()
-                wz_copy(dy, 0).start()
-                wz_copy(dy, 1).start()
-                wf_copy(3 * dy - 2).start()
+            wo_first()
         else:
-            for dy in (1, 3, 2):
-                for up in range(2):
-                    wz_arrival(dy, up).wait_recv()
-                    wf_copy(3 * dy - 1 + up).start()
-    for n in range(10):
-        wf_arrival(n).wait_recv()
+            wo_second()
 
     def piece(ref, who):
         return ref.at[pl.ds(aligned((who // 4) * 16, 16), 16), pl.ds(aligned((who % 4) * lane4, 128), lane4)]
@@ -338,7 +385,7 @@
         each(1, SEQ_DEVS, lambda k: p1_arrival(h, k).wait_recv())
         total = jnp.zeros((16, lane4), F32)
         for k in range(SEQ_DEVS):
-            pe1[h, k] = total.astype(BF16)
+            pe1[h, k] = stb[h] + scale * total
             total = total + pr1[h, k].astype(F32)
         each(1, SEQ_DEVS, lambda k: e1_copy(h, k).start())
         piece(e1.at[h], q)[...] = pe1[h, q]
@@ -378,10 +425,9 @@
     def states(h):
         each(1, SEQ_DEVS, lambda k: e1_arrival(h, k).wait_recv())
         for i in range(4):
-            before = e1[h].astype(F32)
+            shifted = e1[h] + tes[pl.ds(4 * q + i, 1), :]
             if i:
-                before = before + dr1[h, i - 1]
-            shifted = stb[h] + scale * before + tes[pl.ds(4 * q + i, 1), :]
+                shifted = shifted + scale * dr1[h, i - 1]
             mean = jnp.mean(shifted * shifted, axis=1, keepdims=True)
             ns[h, i] = (shifted * lax.rsqrt(mean + NORM_EPS)).astype(BF16)
             for n in (2 * i, 2 * i + 1):
@@ -399,6 +445,7 @@
             sb_copy_in = remote(stb.at[h], stb.at[h], sb_send.at[h, 0], sb_recv.at[h], here)
             sb_copy_in.wait_recv()
 
+    wo_third()
     drift1(0)
     scan1(0)
     drift1(1)
@@ -449,16 +496,16 @@
         return pltpu.make_async_copy(att2_rows(h, q), a2_block(h, q), a2_sem.at[h])
 
     for h in range(2):
-        def attend2(n):
-            sub, head = n // 4, lax.rem(n, 4)
-            rows = pl.ds(aligned(h * 8 * half + sub * 4 * half, 4 * half), 4 * half)
-
+        def attend2(head):
             def cols(p):
                 return pl.ds(aligned(p * gw + head * HEAD_SIZE, HEAD_SIZE), HEAD_SIZE)
 
-            att2[rows, cols(0)] = softmax_mix(qkv2[rows, cols(0)], qkv2[:, cols(1)], qkv2[:, cols(2)])
-
-        each(0, 8, attend2)
+            rows = [pl.ds(h * 8 * half + sub * 4 * half, 4 * half) for sub in range(2)]
+            mixed = [softmax_mix(qkv2[r, cols(0)], qkv2[:, cols(1)], qkv2[:, cols(2)]) for r in rows]
+            for r, m in zip(rows, mixed):
+                att2[r, cols(0)] = m
+
+        each(0, 4, attend2)
         each(1, SEQ_DEVS, lambda k: a2_copy(h, k).start())
         a2_own(h).start()
 
@@ -521,13 +568,15 @@
     each(1, STEP_DEVS, lambda k: te_copy(k).wait_send())
     for dy in range(1, 4):
         sw_copy(dy).wait_send()
-        wy_copy(dy).wait_send()
-        for up in range(2):
-            wz_copy(dy, up).wait_send()
+        for n in range(4):
+            wn_copy(dy, n).wait_send()
     for dy in range(4):
         sw_forward(dy).wait_send()
-    for n in range(10):
+    for n in range(8):
         wf_copy(n).wait_send()
+    for r in range(2):
+        wy_copy(1 + 2 * r).wait_send()
+        wr_copy(r).wait_send()
     each(1, SEQ_DEVS, lambda k: rt_copy(k).wait_send())
 
     @pl.when(q == owner_q)
@@ -580,9 +629,9 @@
             pltpu.VMEM((2, 4, part, width), F32),
             pltpu.VMEM((2, part, width), BF16),
             pltpu.VMEM((2, SEQ_DEVS, 16, lane4), BF16),
-            pltpu.VMEM((2, SEQ_DEVS, 16, lane4), BF16),
-            pltpu.VMEM((2, part, width), BF16),
+            pltpu.VMEM((2, SEQ_DEVS, 16, lane4), F32),
             pltpu.VMEM((2, part, width), F32),
+            pltpu.VMEM((2, 16, lane4), F32),
             pltpu.VMEM((2, 4, part, width), BF16),
             pltpu.VMEM((8 * tok, width), BF16),
             pltpu.VMEM((8 * tok, 3 * INNER // 4), BF16),
@@ -596,7 +645,7 @@
             dma((3,)), dma((3,)), dma, dma((4,)),
             dma((15,)), dma((15,)), dma((3,)), dma((3,)), dma((4,)), dma((4,)), dma((7,)), dma((7,)),
             dma((2, 7)), dma((2,)),
-            dma((3,)), dma((3,)), dma((6,)), dma((6,)), dma((10,)), dma((10,)),
+            dma((3,)), dma((3,)), dma((2,)), dma((2,)), dma((3, 4)), dma((3, 4)), dma((8,)), dma((8,)),
             dma((2, 15)), dma((2, 15)), dma((2, 7)), dma((2, 7)), dma((2, 7)), dma((2, 7)),
             dma((2, 8)), dma((2, 8)), dma((2, 8)), dma((2, 8)),
             dma((2, 7)), dma((2, 7)), dma((2,)), dma((2, 15)), dma((2, 15)), dma((2, 15)), dma((2, 15)),

time: 185 us -> 152 us (0.82)
  Pallas kernels: 181 us -> 147 us
    pallas_call x1, Pallas kernels: 181 us -> 147 us  [on_device(): pl.pallas_call(kernel, out_shape=jax.ShapeDtypeStruct((2, tok, width), F3...]
where the time goes in v3:
time: 152 us; the launch traced here: 151 us
  Pallas kernels  147 us (97%)
  other arithmetic  4.16 us (3%)
    pallas_call x1, Pallas kernels, on_device(): pl.pallas_call(kernel, out_shape=jax.ShapeDtypeStruct((2, tok, width), F3...  147 us

profile of v3, /device:TPU:0, one launch (start us, length us, event | category | flops | bytes accessed | tf_op | source)
XLA Modules:
  0.0 151.2 jit_solution(13687077886707778233)
XLA Ops:
  0.0 0.7 convert_element_type.3
  0.7 0.2 multiply_sine_fusion
  0.8 0.6 pad_maximum_fusion.te_ref
  1.5 0.0 copy-start
  1.5 147.0 %picard.1 = f32[2,128,1536]{2,1,0:T(8,128)} custom-call(f32[2,1536]{1,0:T(2,128)} %pad_maximum_fusion.te_ref, f32[128,1536]{1,0:T(8,128)} %start_ref.1, bf16[1536,6144]{1,0:T(8,128)(2,1)} %wqkv_ref.1, bf16[256,1536]{1,0:T(8,128)(2,1)} %wout_ref.1), custom_call_target="tpu_custom_call" | custom-call | tf_op jit(solution)/shard_map/picard/pallas_call | solution.py:611
  148.5 0.0 copy-done
  148.5 2.7 %multiply_add_fusion = f32[2,128,1536]{2,1,0:T(8,128)} fusion(f32[2,128,1536]{2,1,0:T(8,128)} %picard.1, f32[128,1536]{1,0:T(8,128)S(1)} %copy-done), kind=kLoop, calls=%fused_computation | loop fusion | flops 786432 | bytes 3932160 | tf_op jit(solution)/shard_map/add | solution.py:657
  (1 shorter events, 0.0 us)
Async XLA Ops:
  1.5 147.0 %copy-start = (f32[128,1536]{1,0:T(8,128)S(1)}, f32[128,1536]{1,0:T(8,128)}, u32[]{:S(2)}) copy-start(f32[128,1536]{1,0:T(8,128)} %start_ref.1) | copy-start | bytes 2359300

commit v4 on v3

--- a/solution.py
+++ b/solution.py
@@ -53,8 +53,11 @@
             + jnp.dot(low, weights, preferred_element_type=F32))
 
 
-def softmax_mix(queries, keys, values):
-    scores = lax.dot_general(queries, keys, (((1,), (1,)), ((), ())), preferred_element_type=F32)
+def score(queries, keys):
+    return lax.dot_general(queries, keys, (((1,), (1,)), ((), ())), preferred_element_type=F32)
+
+
+def mix(scores, values):
     expo = jnp.exp2(scores - jnp.max(scores, axis=1, keepdims=True))
     total = jnp.sum(expo, axis=1, keepdims=True)
     mixed = jnp.dot(expo.astype(BF16), values, preferred_element_type=F32)
@@ -65,7 +68,7 @@
     te_ref, start_ref, wqkv_ref, wout_ref,
     out_ref,
     w1, w2, wo, st, tea, tes, swb, rtb, tew, qkv1, att1, recv1, dr1, bs1, pr1, pe1, e1, stb, ns,
-    xs, qkv2, att2, recv2, dr2, bs2, pr2, pe2, e2,
+    xs, qkv2, att2, recv2, dr2, bs2, pr2, pe2, e2, score_a, score_b,
     w1_sem, w2_sem, wo_sem, st_sem,
     te_send, te_recv, sw_send, sw_recv, swf_send, swf_recv, rt_send, rt_recv, sb_send, sb_recv,
     wy_send, wy_recv, wr_send, wr_recv, wn_send, wn_recv, wf_send, wf_recv,
@@ -228,6 +231,8 @@
             wn_copy(2, 2 * r).start()
             wn_copy(2, 2 * r + 1).start()
             wf_copy(3 + r).start()
+
+    def wo_middle():
         for b in (3, 1):
             for n in range(4):
                 wn_arrival(b, n).wait_recv()
@@ -240,8 +245,6 @@
         for n in range(8):
             wf_arrival(n).wait_recv()
 
-    for dy in (1, 3):
-        wy_copy(dy).start()
 
     owner_q = s // 2
     block = s % 2
@@ -298,6 +301,9 @@
     each(1, SEQ_DEVS, lambda k: rt_arrival(k).wait_recv())
     for dy in range(4):
         sw_forwarded(dy).wait_recv()
+
+    for dy in (1, 3):
+        wy_copy(dy).start()
 
     pick_row = lax.broadcasted_iota(jnp.int32, (STEPS, 4 * HEAD_SIZE), 0)
     pick_lane = lax.broadcasted_iota(jnp.int32, (STEPS, 4 * HEAD_SIZE), 1)
@@ -316,6 +322,15 @@
 
     each(0, SEQ_DEVS, build)
 
+    def two_by_two(scores_of, mix_of):
+        def pair(n):
+            score_b[...] = scores_of(2 * n + 1)
+            mix_of(2 * n, score_a[...])
+            score_a[...] = scores_of(jnp.minimum(2 * n + 2, 3))
+            mix_of(2 * n + 1, score_b[...])
+
+        return pair
+
     def a1_copy(h, k):
         return remote(att1.at[h, step_peer(k)], recv1.at[h, :, pl.ds(aligned(s * HEAD_SIZE, 128), HEAD_SIZE)],
                       a1_send.at[h, k - 1], a1_recv.at[h, k - 1], (step_peer(k), q))
@@ -326,24 +341,31 @@
                       a1_send.at[h, k - 1], a1_recv.at[h, k - 1], here)
 
     for h in range(2):
-        def attend1(i):
-            keys = qkv1[i, :, :, HEAD_SIZE:2 * HEAD_SIZE].reshape(8 * tok, HEAD_SIZE)
+        def scores1(i):
+            queries = qkv1[i, :, half * h:half * (h + 1), 0:HEAD_SIZE].reshape(8 * half, HEAD_SIZE)
+            return score(queries, qkv1[i, :, :, HEAD_SIZE:2 * HEAD_SIZE].reshape(8 * tok, HEAD_SIZE))
+
+        def mix1(i, scores):
             values = qkv1[i, :, :, 2 * HEAD_SIZE:3 * HEAD_SIZE].reshape(8 * tok, HEAD_SIZE)
-            mixed = [softmax_mix(qkv1[i, 4 * sub:4 * sub + 4, half * h:half * (h + 1), 0:HEAD_SIZE].reshape(
-                4 * half, HEAD_SIZE), keys, values) for sub in range(2)]
-            for sub in range(2):
-                att1[h, 8 * sub:8 * sub + 8, pl.ds(aligned(i * part, part), part), :] = mixed[sub].reshape(
-                    8, part, HEAD_SIZE)
-
-        each(0, 4, attend1)
-        each(1, STEP_DEVS, lambda k: a1_copy(h, k).start())
-        recv1[h, :, pl.ds(aligned(s * HEAD_SIZE, 128), HEAD_SIZE)] = att1[h, s]
+            att1[h, :, pl.ds(aligned(i * part, part), part), :] = mix(scores, values).reshape(
+                STEP_DEVS, part, HEAD_SIZE)
+
+        attend1 = two_by_two(scores1, mix1)
+        score_a[...] = scores1(0)
         if h == 0:
             wo_own.wait()
             wf_copy(0).start()
+            each(0, 1, attend1)
             wo_first()
+            each(1, 2, attend1)
         else:
+            each(0, 1, attend1)
             wo_second()
+            each(1, 2, attend1)
+        each(1, STEP_DEVS, lambda k: a1_copy(h, k).start())
+        recv1[h, :, pl.ds(aligned(s * HEAD_SIZE, 128), HEAD_SIZE)] = att1[h, s]
+
+    wo_middle()
 
     def piece(ref, who):
         return ref.at[pl.ds(aligned((who // 4) * 16, 16), 16), pl.ds(aligned((who % 4) * lane4, 128), lane4)]
@@ -496,16 +518,19 @@
         return pltpu.make_async_copy(att2_rows(h, q), a2_block(h, q), a2_sem.at[h])
 
     for h in range(2):
-        def attend2(head):
-            def cols(p):
-                return pl.ds(aligned(p * gw + head * HEAD_SIZE, HEAD_SIZE), HEAD_SIZE)
-
-            rows = [pl.ds(h * 8 * half + sub * 4 * half, 4 * half) for sub in range(2)]
-            mixed = [softmax_mix(qkv2[r, cols(0)], qkv2[:, cols(1)], qkv2[:, cols(2)]) for r in rows]
-            for r, m in zip(rows, mixed):
-                att2[r, cols(0)] = m
-
-        each(0, 4, attend2)
+        rows = pl.ds(h * 8 * half, 8 * half)
+
+        def cols(p, head):
+            return pl.ds(aligned(p * gw + head * HEAD_SIZE, HEAD_SIZE), HEAD_SIZE)
+
+        def scores2(head):
+            return score(qkv2[rows, cols(0, head)], qkv2[:, cols(1, head)])
+
+        def mix2(head, scores):
+            att2[rows, cols(0, head)] = mix(scores, qkv2[:, cols(2, head)])
+
+        score_a[...] = scores2(0)
+        each(0, 2, two_by_two(scores2, mix2))
         each(1, SEQ_DEVS, lambda k: a2_copy(h, k).start())
         a2_own(h).start()
 
@@ -642,6 +667,8 @@
             pltpu.VMEM((2, STEP_DEVS, 16, lane4), BF16),
             pltpu.VMEM((2, STEP_DEVS, 16, lane4), F32),
             pltpu.VMEM((2, half, width), F32),
+            pltpu.VMEM((8 * half, 8 * tok), F32),
+            pltpu.VMEM((8 * half, 8 * tok), F32),
             dma((3,)), dma((3,)), dma, dma((4,)),
             dma((15,)), dma((15,)), dma((3,)), dma((3,)), dma((4,)), dma((4,)), dma((7,)), dma((7,)),
             dma((2, 7)), dma((2,)),

time: 152 us -> 140 us (0.921)
  Pallas kernels: 147 us -> 135 us
    pallas_call x1, Pallas kernels: 147 us -> 135 us  [on_device(): pl.pallas_call(kernel, out_shape=jax.ShapeDtypeStruct((2, tok, width), F3...]
where the time goes in v4:
time: 140 us; the launch traced here: 139 us
  Pallas kernels  135 us (96%)
  other arithmetic  4.16 us (3%)
    pallas_call x1, Pallas kernels, on_device(): pl.pallas_call(kernel, out_shape=jax.ShapeDtypeStruct((2, tok, width), F3...  135 us

profile of v4, /device:TPU:0, one launch (start us, length us, event | category | flops | bytes accessed | tf_op | source)
XLA Modules:
  0.0 139.1 jit_solution(4653896051826356646)
XLA Ops:
  0.0 0.7 convert_element_type.3
  0.7 0.2 multiply_sine_fusion
  0.8 0.6 pad_maximum_fusion.te_ref
  1.5 0.0 copy-start
  1.5 134.9 %picard.1 = f32[2,128,1536]{2,1,0:T(8,128)} custom-call(f32[2,1536]{1,0:T(2,128)} %pad_maximum_fusion.te_ref, f32[128,1536]{1,0:T(8,128)} %start_ref.1, bf16[1536,6144]{1,0:T(8,128)(2,1)} %wqkv_ref.1, bf16[256,1536]{1,0:T(8,128)(2,1)} %wout_ref.1), custom_call_target="tpu_custom_call" | custom-call | tf_op jit(solution)/shard_map/picard/pallas_call | solution.py:636
  136.3 0.0 copy-done
  136.3 2.7 %multiply_add_fusion = f32[2,128,1536]{2,1,0:T(8,128)} fusion(f32[2,128,1536]{2,1,0:T(8,128)} %picard.1, f32[128,1536]{1,0:T(8,128)S(1)} %copy-done), kind=kLoop, calls=%fused_computation | loop fusion | flops 786432 | bytes 3932160 | tf_op jit(solution)/shard_map/add | solution.py:684
  (1 shorter events, 0.0 us)
Async XLA Ops:
  1.5 134.9 %copy-start = (f32[128,1536]{1,0:T(8,128)S(1)}, f32[128,1536]{1,0:T(8,128)}, u32[]{:S(2)}) copy-start(f32[128,1536]{1,0:T(8,128)} %start_ref.1) | copy-start | bytes 2359300

commit v5 on v4

--- a/solution.py
+++ b/solution.py
@@ -469,10 +469,10 @@
 
     wo_third()
     drift1(0)
+    drift1(1)
     scan1(0)
-    drift1(1)
+    scan1(1)
     states(0)
-    scan1(1)
     states(1)
 
     for n in range(3):
@@ -584,8 +584,8 @@
                 out_ref[i, half * b + part * h:half * b + part * (h + 1), :] = e2[h, rows, :] + dr2[h, i, rows, :]
 
     drift2(0)
+    drift2(1)
     scan2(0)
-    drift2(1)
     scan2(1)
     finish(0)
     finish(1)

time: 140 us -> 133 us (0.950)
  Pallas kernels: 135 us -> 127 us
    pallas_call x1, Pallas kernels: 135 us -> 127 us  [on_device(): pl.pallas_call(kernel, out_shape=jax.ShapeDtypeStruct((2, tok, width), F3...]
where the time goes in v5:
time: 133 us; the launch traced here: 132 us
  Pallas kernels  127 us (95%)
  other arithmetic  4.16 us (3%)
    pallas_call x1, Pallas kernels, on_device(): pl.pallas_call(kernel, out_shape=jax.ShapeDtypeStruct((2, tok, width), F3...  127 us
    add x1, other arithmetic, on_device(): return start_state[None] + 1.0 / STEPS * sums  2.72 us

profile of v5, /device:TPU:0, one launch (start us, length us, event | category | flops | bytes accessed | tf_op | source)
XLA Modules:
  0.0 131.7 jit_solution(9153774023225135594)
XLA Ops:
  0.0 0.7 convert_element_type.3
  0.7 0.2 multiply_sine_fusion
  0.8 0.6 pad_maximum_fusion.te_ref
  1.5 0.0 copy-start
  1.5 127.5 %picard.1 = f32[2,128,1536]{2,1,0:T(8,128)} custom-call(f32[2,1536]{1,0:T(2,128)} %pad_maximum_fusion.te_ref, f32[128,1536]{1,0:T(8,128)} %start_ref.1, bf16[1536,6144]{1,0:T(8,128)(2,1)} %wqkv_ref.1, bf16[256,1536]{1,0:T(8,128)(2,1)} %wout_ref.1), custom_call_target="tpu_custom_call" | custom-call | tf_op jit(solution)/shard_map/picard/pallas_call | solution.py:636
  128.9 0.0 copy-done
  128.9 2.7 %multiply_add_fusion = f32[2,128,1536]{2,1,0:T(8,128)} fusion(f32[2,128,1536]{2,1,0:T(8,128)} %picard.1, f32[128,1536]{1,0:T(8,128)S(1)} %copy-done), kind=kLoop, calls=%fused_computation | loop fusion | flops 786432 | bytes 3932160 | tf_op jit(solution)/shard_map/add | solution.py:684
  (1 shorter events, 0.0 us)
Async XLA Ops:
  1.5 127.5 %copy-start = (f32[128,1536]{1,0:T(8,128)S(1)}, f32[128,1536]{1,0:T(8,128)}, u32[]{:S(2)}) copy-start(f32[128,1536]{1,0:T(8,128)} %start_ref.1) | copy-start | bytes 2359300

commit v6 on v5

--- a/solution.py
+++ b/solution.py
@@ -478,8 +478,8 @@
     for n in range(3):
         w2_copy(n).wait()
 
-    def project(h, sub):
-        rows = pl.ds(h * 8 * half + sub * 4 * half, 4 * half)
+    def project(h):
+        rows = pl.ds(h * 8 * half, 8 * half)
 
         def columns(n):
             cols = pl.ds(aligned(n * gw, gw), gw)
@@ -489,33 +489,32 @@
         each(0, 3, columns)
 
     for h in range(2):
-        for sub in range(2):
-            for m in range(4 * sub, 4 * sub + 4):
-                x_arrival(h, m).wait()
-                x_forward(h, m).start()
-        for sub in range(2):
-            for m in range(4 * sub, 4 * sub + 4):
-                x_forwarded(h, m).wait_recv()
-            project(h, sub)
-
-    def a2_block(h, who):
+        for m in range(8):
+            x_arrival(h, m).wait()
+            x_forward(h, m).start()
+        for m in range(8):
+            x_forwarded(h, m).wait_recv()
+        project(h)
+
+    def a2_block(h, p, who):
         yy, cc = who // 2, who % 2
         return recv2.at[h, pl.ds(aligned((yy // 2) * half, half), half),
-                        pl.ds(aligned(((yy % 2) * 2 + cc) * gw, gw), gw)]
-
-    def att2_rows(h, who):
-        return att2.at[pl.ds(aligned(h * 8 * half + who * half, half), half)]
-
-    def a2_copy(h, k):
+                        pl.ds(aligned(((yy % 2) * 2 + cc) * gw + p * (gw // 2), gw // 2), gw // 2)]
+
+    def att2_rows(h, p, who):
+        return att2.at[pl.ds(aligned(h * 8 * half + who * half, half), half), pl.ds(p * (gw // 2), gw // 2)]
+
+    def a2_copy(h, p, k):
         dest = seq_peer(k)
-        return remote(att2_rows(h, dest), a2_block(h, q), a2_send.at[h, k - 1], a2_recv.at[h, k - 1], (s, dest))
-
-    def a2_arrival(h, k):
-        return remote(att2_rows(h, q), a2_block(h, seq_peer(SEQ_DEVS - k)),
-                      a2_send.at[h, k - 1], a2_recv.at[h, k - 1], here)
-
-    def a2_own(h):
-        return pltpu.make_async_copy(att2_rows(h, q), a2_block(h, q), a2_sem.at[h])
+        return remote(att2_rows(h, p, dest), a2_block(h, p, q), a2_send.at[h, p, k - 1], a2_recv.at[h, p, k - 1],
+                      (s, dest))
+
+    def a2_arrival(h, p, k):
+        return remote(att2_rows(h, p, q), a2_block(h, p, seq_peer(SEQ_DEVS - k)),
+                      a2_send.at[h, p, k - 1], a2_recv.at[h, p, k - 1], here)
+
+    def a2_own(h, p):
+        return pltpu.make_async_copy(att2_rows(h, p, q), a2_block(h, p, q), a2_sem.at[h, p])
 
     for h in range(2):
         rows = pl.ds(h * 8 * half, 8 * half)
@@ -530,9 +529,10 @@
             att2[rows, cols(0, head)] = mix(scores, qkv2[:, cols(2, head)])
 
         score_a[...] = scores2(0)
-        each(0, 2, two_by_two(scores2, mix2))
-        each(1, SEQ_DEVS, lambda k: a2_copy(h, k).start())
-        a2_own(h).start()
+        for p in range(2):
+            each(p, p + 1, two_by_two(scores2, mix2))
+            each(1, SEQ_DEVS, lambda k: a2_copy(h, p, k).start())
+            a2_own(h, p).start()
 
     def p2_copy(h, k):
         dest = step_peer(k)
@@ -551,8 +551,9 @@
                       e2_send.at[h, k - 1], e2_recv.at[h, k - 1], here)
 
     def drift2(h):
-        a2_own(h).wait()
-        each(1, SEQ_DEVS, lambda k: a2_arrival(h, k).wait_recv())
+        for p in range(2):
+            a2_own(h, p).wait()
+            each(1, SEQ_DEVS, lambda k: a2_arrival(h, p, k).wait_recv())
 
         def tile(n):
             cols = pl.ds(aligned(n * 256, 256), 256)
@@ -613,7 +614,8 @@
         for k in range(1, SEQ_DEVS):
             p1_copy(h, k).wait_send()
             e1_copy(h, k).wait_send()
-            a2_copy(h, k).wait_send()
+            for p in range(2):
+                a2_copy(h, p, k).wait_send()
         for k in range(1, STEP_DEVS):
             a1_copy(h, k).wait_send()
             p2_copy(h, k).wait_send()
@@ -675,7 +677,7 @@
             dma((3,)), dma((3,)), dma((2,)), dma((2,)), dma((3, 4)), dma((3, 4)), dma((8,)), dma((8,)),
             dma((2, 15)), dma((2, 15)), dma((2, 7)), dma((2, 7)), dma((2, 7)), dma((2, 7)),
             dma((2, 8)), dma((2, 8)), dma((2, 8)), dma((2, 8)),
-            dma((2, 7)), dma((2, 7)), dma((2,)), dma((2, 15)), dma((2, 15)), dma((2, 15)), dma((2, 15)),
+            dma((2, 2, 7)), dma((2, 2, 7)), dma((2, 2)), dma((2, 15)), dma((2, 15)), dma((2, 15)), dma((2, 15)),
         ],
         compiler_params=pltpu.CompilerParams(
             collective_id=0, has_side_effects=True, vmem_limit_bytes=58 * 1024 * 1024),

time: 133 us -> 131 us (0.985)
  no operation moved by 1% of the time
where the time goes in v6:
time: 131 us
  Pallas kernels  126 us (96%)
  other arithmetic  4.16 us (3%)
    pallas_call x1, Pallas kernels, on_device(): pl.pallas_call(kernel, out_shape=jax.ShapeDtypeStruct((2, tok, width), F3...  126 us
    add x1, other arithmetic, on_device(): return start_state[None] + 1.0 / STEPS * sums  2.72 us

profile of v6, /device:TPU:0, one launch (start us, length us, event | category | flops | bytes accessed | tf_op | source)
XLA Modules:
  0.0 130.6 jit_solution(9900211454144614825)
XLA Ops:
  0.0 0.7 convert_element_type.3
  0.7 0.2 multiply_sine_fusion
  0.8 0.6 pad_maximum_fusion.te_ref
  1.5 0.0 copy-start
  1.5 126.4 %picard.1 = f32[2,128,1536]{2,1,0:T(8,128)} custom-call(f32[2,1536]{1,0:T(2,128)} %pad_maximum_fusion.te_ref, f32[128,1536]{1,0:T(8,128)} %start_ref.1, bf16[1536,6144]{1,0:T(8,128)(2,1)} %wqkv_ref.1, bf16[256,1536]{1,0:T(8,128)(2,1)} %wout_ref.1), custom_call_target="tpu_custom_call" | custom-call | tf_op jit(solution)/shard_map/picard/pallas_call | solution.py:638
  127.9 0.0 copy-done
  127.9 2.7 %multiply_add_fusion = f32[2,128,1536]{2,1,0:T(8,128)} fusion(f32[2,128,1536]{2,1,0:T(8,128)} %picard.1, f32[128,1536]{1,0:T(8,128)S(1)} %copy-done), kind=kLoop, calls=%fused_computation | loop fusion | flops 786432 | bytes 3932160 | tf_op jit(solution)/shard_map/add | solution.py:686
  (1 shorter events, 0.0 us)
Async XLA Ops:
  1.5 126.5 %copy-start = (f32[128,1536]{1,0:T(8,128)S(1)}, f32[128,1536]{1,0:T(8,128)}, u32[]{:S(2)}) copy-start(f32[128,1536]{1,0:T(8,128)} %start_ref.1) | copy-start | bytes 2359300
